TPU v7x, 32 devices: a whole 2x2x4 slice. The times are simulated.
32 devices in a mesh: dp: 8 (over y, x, core), tensor: 4 (over z).
Axes of the slice: x: 2, y: 2, z: 4, core: 2. Of those that a mesh axis runs over, the one named last changes fastest.
Arguments:
- block_input: bfloat16 [16384, 1024], P(('dp', 'tensor')), may hold values from -6 to 6
- ln1_gain: bfloat16 [1024], P(('dp', 'tensor')), may hold values from 0.5 to 1.5
- ln1_bias: bfloat16 [1024], P(('dp', 'tensor')), may hold values from -1.5 to 1.5
- w_query: bfloat16 [1024, 1024], P('dp', 'tensor'), may hold values from -0.1875 to 0.1875
- w_key: bfloat16 [1024, 1024], P('dp', 'tensor'), may hold values from -0.1875 to 0.1875
- w_value: bfloat16 [1024, 1024], P('dp', 'tensor'), may hold values from -0.1875 to 0.1875
- query_bias: bfloat16 [1024], P(('dp', 'tensor')), may hold values from -1.5 to 1.5
- value_bias: bfloat16 [1024], P(('dp', 'tensor')), may hold values from -1.5 to 1.5
- w_dense: bfloat16 [1024, 1024], P('tensor', 'dp'), may hold values from -0.5 to 0.5
- dense_bias: bfloat16 [1024], P(('dp', 'tensor')), may hold values from -1.5 to 1.5
- ln2_gain: bfloat16 [1024], P(('dp', 'tensor')), may hold values from 0.5 to 1.5
- ln2_bias: bfloat16 [1024], P(('dp', 'tensor')), may hold values from -1.5 to 1.5
- w_fc1: bfloat16 [1024, 4096], P('dp', 'tensor'), may hold values from -0.1875 to 0.1875
- fc1_bias: bfloat16 [4096], P(('dp', 'tensor')), may hold values from -1.5 to 1.5
- w_fc2: bfloat16 [4096, 1024], P('tensor', 'dp'), may hold values from -0.09375 to 0.09375
- fc2_bias: bfloat16 [1024], P(('dp', 'tensor')), may hold values from -1.5 to 1.5
- out_grad: bfloat16 [16384, 1024], P(('dp', 'tensor')), may hold values from -6 to 6
- doc_lengths: int32 [8, 8], P('dp'), may hold values from 1 to 512, 2048 in all within a row
Outputs:
- block_output: bfloat16 [16384, 1024], P(('dp', 'tensor'))
- input_grad: float32 [16384, 1024], P(('dp', 'tensor'))
- ln1_gain_grad: float32 [1024], P(('dp', 'tensor'))
- ln1_bias_grad: float32 [1024], P(('dp', 'tensor'))
- w_query_grad: float32 [1024, 1024], P('dp', 'tensor')
- w_key_grad: float32 [1024, 1024], P('dp', 'tensor')
- w_value_grad: float32 [1024, 1024], P('dp', 'tensor')
- query_bias_grad: float32 [1024], P(('dp', 'tensor'))
- value_bias_grad: float32 [1024], P(('dp', 'tensor'))
- w_dense_grad: float32 [1024, 1024], P('tensor', 'dp')
- dense_bias_grad: float32 [1024], P(('dp', 'tensor'))
- ln2_gain_grad: float32 [1024], P(('dp', 'tensor'))
- ln2_bias_grad: float32 [1024], P(('dp', 'tensor'))
- w_fc1_grad: float32 [1024, 4096], P('dp', 'tensor')
- fc1_bias_grad: float32 [4096], P(('dp', 'tensor'))
- w_fc2_grad: float32 [4096, 1024], P('tensor', 'dp')
- fc2_bias_grad: float32 [1024], P(('dp', 'tensor'))
Inputs may be any that keep to these rules, and one draw needn't show every extreme that they name: `doc_lengths`: each packed row of 2048 tokens holds 8 documents whose lengths sum to 2048, the longest exactly 512.
All inputs are finite; a program needn't handle non-finite values.
Results may differ from a plain program's by a relative error of at most 0.018.
Values may be sent and summed in bfloat16 or wider, within the bound.
A program may use at most 192 MiB of HBM per device.

v0:
```python
import jax
import jax.numpy as jnp
from jax import lax
from jax.sharding import PartitionSpec as P

H = 16
HD = 64


EPSILON = 1e-05
MASK_VALUE = -1e30


def layer_norm(values, gain, shift):
    center = jnp.mean(values, axis=-1, keepdims=True)
    centered = values - center
    spread = jnp.mean(centered * centered, axis=-1, keepdims=True)
    return centered * lax.rsqrt(spread + EPSILON) * gain + shift


def gelu_tanh(values):
    return jax.nn.gelu(values, approximate=True)


def fetch_weights(w_query, w_key, w_value, w_fc1, w_dense, w_fc2):
    row_part = (
        lax.all_gather(w_query, "dp", axis=0, tiled=True),
        lax.all_gather(w_key, "dp", axis=0, tiled=True),
        lax.all_gather(w_value, "dp", axis=0, tiled=True),
        lax.all_gather(w_fc1, "dp", axis=0, tiled=True),
    )
    col_part = (
        lax.all_gather(w_dense, "dp", axis=1, tiled=True),
        lax.all_gather(w_fc2, "dp", axis=1, tiled=True),
    )
    return (row_part[0], row_part[1], row_part[2], row_part[3], col_part[0], col_part[1])


def block_scores(query_block, key_block, first_row, segment, slopes):
    block_rows = query_block.shape[0]
    key_count = key_block.shape[0]
    raw = jnp.einsum("qhd,khd->hqk", query_block, key_block, preferred_element_type=jnp.float32)
    query_rows = first_row + jnp.arange(block_rows, dtype=jnp.int32)
    key_rows = jnp.arange(key_count, dtype=jnp.int32)
    query_segment = lax.dynamic_slice_in_dim(segment, first_row, block_rows)
    allowed = (key_rows[None, :] <= query_rows[:, None]) & (
        segment[None, :] == query_segment[:, None]
    )
    distance = (query_rows[:, None] - key_rows[None, :]).astype(jnp.float32)
    scores = raw * query_block.shape[2] ** (-0.5) - slopes[:, None, None] * distance[None]
    return jnp.where(allowed[None], scores, MASK_VALUE)


def per_device(
    block_input,
    ln1_gain,
    ln1_bias,
    w_query,
    w_key,
    w_value,
    query_bias,
    value_bias,
    w_dense,
    dense_bias,
    ln2_gain,
    ln2_bias,
    w_fc1,
    fc1_bias,
    w_fc2,
    fc2_bias,
    out_grad,
    doc_lengths,
):
    vectors = (
        lax.all_gather(ln1_gain, ("dp", "tensor"), axis=0, tiled=True),
        lax.all_gather(ln1_bias, ("dp", "tensor"), axis=0, tiled=True),
        lax.all_gather(query_bias, ("dp", "tensor"), axis=0, tiled=True),
        lax.all_gather(value_bias, ("dp", "tensor"), axis=0, tiled=True),
        lax.all_gather(dense_bias, ("dp", "tensor"), axis=0, tiled=True),
        lax.all_gather(ln2_gain, ("dp", "tensor"), axis=0, tiled=True),
        lax.all_gather(ln2_bias, ("dp", "tensor"), axis=0, tiled=True),
        lax.all_gather(fc1_bias, ("dp", "tensor"), axis=0, tiled=True),
        lax.all_gather(fc2_bias, ("dp", "tensor"), axis=0, tiled=True),
    )
    (
        gain_first,
        shift_first,
        query_shift_all,
        value_shift_all,
        dense_shift,
        gain_second,
        shift_second,
        hidden_shift_all,
        output_shift,
    ) = [vector.astype(jnp.float32) for vector in vectors]
    query_full, key_full, value_full, fc1_full, dense_full, fc2_full = fetch_weights(
        w_query, w_key, w_value, w_fc1, w_dense, w_fc2
    )
    head_width = query_full.shape[1]
    hidden_width = fc1_full.shape[1]
    local_rows = block_input.shape[0]
    total_rows = local_rows * lax.axis_size("tensor")
    tensor_place = lax.axis_index("tensor")
    query_shift = lax.dynamic_slice_in_dim(query_shift_all, tensor_place * head_width, head_width)
    value_shift = lax.dynamic_slice_in_dim(value_shift_all, tensor_place * head_width, head_width)
    hidden_shift = lax.dynamic_slice_in_dim(
        hidden_shift_all, tensor_place * hidden_width, hidden_width
    )
    local_heads = head_width // HD
    head_ids = tensor_place * local_heads + jnp.arange(local_heads, dtype=jnp.int32)
    slopes = 2.0 ** (-8.0 * (head_ids.astype(jnp.float32) + 1.0) / H)
    doc_ends = jnp.cumsum(doc_lengths[0])
    places = jnp.arange(total_rows, dtype=jnp.int32)
    segment = jnp.sum((places[:, None] >= doc_ends[None, :]).astype(jnp.int32), axis=1)
    block_rows = min(512, total_rows)
    block_count = total_rows // block_rows
    rows_in = block_input.astype(jnp.float32)
    gathered_first = lax.all_gather(
        layer_norm(rows_in, gain_first, shift_first).astype(jnp.bfloat16),
        "tensor",
        axis=0,
        tiled=True,
    )
    query = (
        jnp.dot(gathered_first, query_full, preferred_element_type=jnp.float32) + query_shift
    ).astype(jnp.bfloat16)
    keys_local = jnp.dot(gathered_first, key_full, preferred_element_type=jnp.float32).astype(
        jnp.bfloat16
    )
    values_local = (
        jnp.dot(gathered_first, value_full, preferred_element_type=jnp.float32) + value_shift
    ).astype(jnp.bfloat16)
    query_heads = query.reshape(total_rows, local_heads, HD)
    key_heads = keys_local.reshape(total_rows, local_heads, HD)
    value_heads = values_local.reshape(total_rows, local_heads, HD)

    def forward_block(block_index):
        first_row = block_index * block_rows
        query_block = lax.dynamic_slice_in_dim(query_heads, first_row, block_rows)
        scores = block_scores(query_block, key_heads, first_row, segment, slopes)
        highest = jnp.max(scores, axis=-1, keepdims=True)
        weights = jnp.exp(scores - highest)
        mass_sum = jnp.sum(weights, axis=-1, keepdims=True)
        probs = (weights / mass_sum).astype(jnp.bfloat16)
        result = jnp.einsum("hqk,khd->qhd", probs, value_heads, preferred_element_type=jnp.float32)
        return (result.astype(jnp.bfloat16), (highest + jnp.log(mass_sum))[..., 0])

    attended, log_mass = lax.map(forward_block, jnp.arange(block_count, dtype=jnp.int32))
    attended = attended.reshape(total_rows, head_width)
    attn_sum = lax.psum_scatter(
        jnp.dot(attended, dense_full, preferred_element_type=jnp.float32).astype(jnp.bfloat16),
        "tensor",
        scatter_dimension=0,
        tiled=True,
    ).astype(jnp.float32)
    mixed = rows_in + attn_sum + dense_shift
    gathered_second = lax.all_gather(
        layer_norm(mixed, gain_second, shift_second).astype(jnp.bfloat16),
        "tensor",
        axis=0,
        tiled=True,
    )
    pre_act = jnp.dot(gathered_second, fc1_full, preferred_element_type=jnp.float32) + hidden_shift
    active = gelu_tanh(pre_act).astype(jnp.bfloat16)
    ffn_sum = lax.psum_scatter(
        jnp.dot(active, fc2_full, preferred_element_type=jnp.float32).astype(jnp.bfloat16),
        "tensor",
        scatter_dimension=0,
        tiled=True,
    ).astype(jnp.float32)
    block_output = (mixed + ffn_sum + output_shift).astype(jnp.bfloat16)
    query_full, key_full, value_full, fc1_full, dense_full, fc2_full = fetch_weights(
        w_query, w_key, w_value, w_fc1, w_dense, w_fc2
    )
    grad_output = out_grad.astype(jnp.float32)
    grad_output_shift = jnp.sum(grad_output, axis=0)
    grad_ffn = lax.all_gather(grad_output.astype(jnp.bfloat16), "tensor", axis=0, tiled=True)
    grad_fc2 = jnp.einsum("rf,rd->fd", active, grad_ffn, preferred_element_type=jnp.float32)
    grad_active = jnp.einsum("rd,fd->rf", grad_ffn, fc2_full, preferred_element_type=jnp.float32)
    unused_value, gelu_pull = jax.vjp(gelu_tanh, pre_act)
    grad_pre = gelu_pull(grad_active)[0].astype(jnp.bfloat16)
    grad_fc1 = jnp.einsum(
        "rd,rf->df", gathered_second, grad_pre, preferred_element_type=jnp.float32
    )
    grad_hidden_local = jnp.sum(grad_pre.astype(jnp.float32), axis=0)
    grad_mid = lax.psum_scatter(
        jnp.einsum("rf,df->rd", grad_pre, fc1_full, preferred_element_type=jnp.float32).astype(
            jnp.bfloat16
        ),
        "tensor",
        scatter_dimension=0,
        tiled=True,
    ).astype(jnp.float32)
    unused_second, second_pull = jax.vjp(layer_norm, mixed, gain_second, shift_second)
    grad_mixed_norm, grad_gain_second, grad_shift_second = second_pull(grad_mid)
    grad_mixed = grad_output + grad_mixed_norm
    grad_dense_shift = jnp.sum(grad_mixed, axis=0)
    grad_attn = lax.all_gather(grad_mixed.astype(jnp.bfloat16), "tensor", axis=0, tiled=True)
    grad_dense = jnp.einsum("rc,rd->cd", attended, grad_attn, preferred_element_type=jnp.float32)
    grad_attended = jnp.einsum(
        "rd,cd->rc", grad_attn, dense_full, preferred_element_type=jnp.float32
    ).astype(jnp.bfloat16)
    grad_attended = grad_attended.reshape(total_rows, local_heads, HD)

    def backward_block(carried, block_index):
        grad_keys_sum, grad_values_sum = carried
        first_row = block_index * block_rows
        query_block = lax.dynamic_slice_in_dim(query_heads, first_row, block_rows)
        scores = block_scores(query_block, key_heads, first_row, segment, slopes)
        block_lse = lax.dynamic_index_in_dim(log_mass, block_index, keepdims=False)
        probs = jnp.exp(scores - block_lse[..., None])
        grad_block = lax.dynamic_slice_in_dim(grad_attended, first_row, block_rows)
        grad_probs = jnp.einsum(
            "qhd,khd->hqk", grad_block, value_heads, preferred_element_type=jnp.float32
        )
        weighted = jnp.sum(probs * grad_probs, axis=-1, keepdims=True)
        grad_scores = (probs * (grad_probs - weighted)).astype(jnp.bfloat16)
        scale_factor = query_block.shape[2] ** (-0.5)
        grad_query_block = (
            jnp.einsum("hqk,khd->qhd", grad_scores, key_heads, preferred_element_type=jnp.float32)
            * scale_factor
        )
        grad_key_block = (
            jnp.einsum("hqk,qhd->khd", grad_scores, query_block, preferred_element_type=jnp.float32)
            * scale_factor
        )
        grad_value_block = jnp.einsum(
            "hqk,qhd->khd",
            probs.astype(jnp.bfloat16),
            grad_block,
            preferred_element_type=jnp.float32,
        )
        grad_keys_sum = grad_keys_sum + grad_key_block
        grad_values_sum = grad_values_sum + grad_value_block
        return ((grad_keys_sum, grad_values_sum), grad_query_block.astype(jnp.bfloat16))

    zero_heads = jnp.zeros((total_rows, local_heads, HD), jnp.float32)
    (grad_keys_sum, grad_values_sum), grad_query = lax.scan(
        backward_block, (zero_heads, zero_heads), jnp.arange(block_count, dtype=jnp.int32)
    )
    grad_query = grad_query.reshape(total_rows, head_width)
    grad_keys = grad_keys_sum.astype(jnp.bfloat16).reshape(total_rows, head_width)
    grad_values = grad_values_sum.astype(jnp.bfloat16).reshape(total_rows, head_width)
    grad_query_w = jnp.einsum(
        "rd,rc->dc", gathered_first, grad_query, preferred_element_type=jnp.float32
    )
    grad_key_w = jnp.einsum(
        "rd,rc->dc", gathered_first, grad_keys, preferred_element_type=jnp.float32
    )
    grad_value_w = jnp.einsum(
        "rd,rc->dc", gathered_first, grad_values, preferred_element_type=jnp.float32
    )
    grad_query_shift = lax.dynamic_update_slice_in_dim(
        jnp.zeros_like(query_shift_all),
        jnp.sum(grad_query.astype(jnp.float32), axis=0),
        tensor_place * head_width,
        0,
    )
    grad_value_shift = lax.dynamic_update_slice_in_dim(
        jnp.zeros_like(value_shift_all),
        jnp.sum(grad_values.astype(jnp.float32), axis=0),
        tensor_place * head_width,
        0,
    )
    grad_hidden_shift = lax.dynamic_update_slice_in_dim(
        jnp.zeros_like(hidden_shift_all), grad_hidden_local, tensor_place * hidden_width, 0
    )
    total_term = jnp.einsum("rc,dc->rd", grad_query, query_full, preferred_element_type=jnp.float32)
    total_term = total_term + jnp.einsum(
        "rc,dc->rd", grad_keys, key_full, preferred_element_type=jnp.float32
    )
    grad_normed = lax.psum_scatter(
        (
            total_term
            + jnp.einsum("rc,dc->rd", grad_values, value_full, preferred_element_type=jnp.float32)
        ).astype(jnp.bfloat16),
        "tensor",
        scatter_dimension=0,
        tiled=True,
    ).astype(jnp.float32)
    unused_first, first_pull = jax.vjp(layer_norm, rows_in, gain_first, shift_first)
    grad_rows_norm, grad_gain_first, grad_shift_first = first_pull(grad_normed)
    input_grad = grad_mixed + grad_rows_norm
    row_grads = (
        lax.psum_scatter(grad_query_w, "dp", scatter_dimension=0, tiled=True),
        lax.psum_scatter(grad_key_w, "dp", scatter_dimension=0, tiled=True),
        lax.psum_scatter(grad_value_w, "dp", scatter_dimension=0, tiled=True),
        lax.psum_scatter(grad_fc1, "dp", scatter_dimension=0, tiled=True),
    )
    col_grads = (
        lax.psum_scatter(grad_dense, "dp", scatter_dimension=1, tiled=True),
        lax.psum_scatter(grad_fc2, "dp", scatter_dimension=1, tiled=True),
    )
    vector_grads = (
        lax.psum_scatter(grad_gain_first, ("dp", "tensor"), scatter_dimension=0, tiled=True),
        lax.psum_scatter(grad_shift_first, ("dp", "tensor"), scatter_dimension=0, tiled=True),
        lax.psum_scatter(grad_query_shift, ("dp", "tensor"), scatter_dimension=0, tiled=True),
        lax.psum_scatter(grad_value_shift, ("dp", "tensor"), scatter_dimension=0, tiled=True),
        lax.psum_scatter(grad_dense_shift, ("dp", "tensor"), scatter_dimension=0, tiled=True),
        lax.psum_scatter(grad_gain_second, ("dp", "tensor"), scatter_dimension=0, tiled=True),
        lax.psum_scatter(grad_shift_second, ("dp", "tensor"), scatter_dimension=0, tiled=True),
        lax.psum_scatter(grad_hidden_shift, ("dp", "tensor"), scatter_dimension=0, tiled=True),
        lax.psum_scatter(grad_output_shift, ("dp", "tensor"), scatter_dimension=0, tiled=True),
    )
    return (
        block_output,
        input_grad,
        vector_grads[0],
        vector_grads[1],
        row_grads[0],
        row_grads[1],
        row_grads[2],
        vector_grads[2],
        vector_grads[3],
        col_grads[0],
        vector_grads[4],
        vector_grads[5],
        vector_grads[6],
        row_grads[3],
        vector_grads[7],
        col_grads[1],
        vector_grads[8],
    )


def solution(mesh):
    placed = (
        P(("dp", "tensor"), None),
        P(("dp", "tensor")),
        P(("dp", "tensor")),
        P("dp", "tensor"),
        P("dp", "tensor"),
        P("dp", "tensor"),
        P(("dp", "tensor")),
        P(("dp", "tensor")),
        P("tensor", "dp"),
        P(("dp", "tensor")),
        P(("dp", "tensor")),
        P(("dp", "tensor")),
        P("dp", "tensor"),
        P(("dp", "tensor")),
        P("tensor", "dp"),
        P(("dp", "tensor")),
        P(("dp", "tensor"), None),
        P("dp", None),
    )
    return jax.shard_map(
        per_device,
        mesh=mesh,
        in_specs=placed,
        out_specs=(
            P(("dp", "tensor"), None),
            P(("dp", "tensor"), None),
            P(("dp", "tensor")),
            P(("dp", "tensor")),
            P("dp", "tensor"),
            P("dp", "tensor"),
            P("dp", "tensor"),
            P(("dp", "tensor")),
            P(("dp", "tensor")),
            P("tensor", "dp"),
            P(("dp", "tensor")),
            P(("dp", "tensor")),
            P(("dp", "tensor")),
            P("dp", "tensor"),
            P(("dp", "tensor")),
            P("tensor", "dp"),
            P(("dp", "tensor")),
        ),
        check_vma=False,
    )
```

profile of v0, /device:TPU:0, one launch (start us, length us, event | category | flops | bytes accessed | tf_op | source)
XLA Modules:
  0.0 1386.9 jit_solution(1732297161509697171)
XLA Ops:
  18.0 42.2 %all-reduce.18 = (bf16[1024]{0:T(1024)(128)(2,1)}, bf16[1024]{0:T(1024)(128)(2,1)}, bf16[1024]{0:T(1024)(128)(2,1)S(1)}, bf16[1024]{0:T(1024)(128)(2,1)S(1)}, bf...) all-reduce(bf16[1024]{0:T(1024)(128)(2,1)S(1)} %dynamic-update-slic, ...), channel_id=1, replica_groups=mesh['dp'=8,'tensor'=4] {'dp','tensor'}, use_global_device_ids=true, to_apply=%add.6 | all-reduce | flops 8192 | bytes 32768
  104.0 40.8 %all-gather.8.cloned.1.call-done = bf16[2048,1024]{1,0:T(8,128)(2,1)} async-done(((bf16[512,1024]{1,0:T(8,128)(2,1)}), bf16[2048,1024]{1,0:T(8,128)(2,1)}) %all-gather.8.cloned.1.call-update) | async-done | bytes 4194320 | tf_op jit(solution)/shard_map/all_gather | solution.py:118
  154.1 98.8 %while.28 = (s32[]{:T(128)}, bf16[4,512,4,64]{1,3,2,0:T(8,128)(2,1)S(1)}, f32[4,4,512]{2,1,0:T(4,128)S(1)}, s32[4]{0:T(128)S(1)}, s32[2048]{0:T(1024)S(1)}, /*in...) while((s32[]{:T(128)}, ...), condition=%wide.region_7.8_spmd.clone, body=%wide.region_4.7_spmd.clone.sunk | while | flops 1154611712 | bytes 90788640 | solution.py:148
  258.9 74.7 %reduce-scatter.11.cloned.1.call-done = bf16[512,1024]{1,0:T(8,128)(2,1)} async-done(((bf16[2048,1024]{1,0:T(8,128)(2,1)}), bf16[512,1024]{1,0:T(8,128)(2,1)}) %reduce-scatter.11.cloned.1.call-update) | async-done | bytes 1048592 | tf_op jit(solution)/shard_map/reduce_scatter | solution.py:150
  340.2 67.9 %all-gather = bf16[32,1,128]{2,1,0:T(2,128)(2,1)S(1)} all-gather(bf16[1,1,128]{2,1,0:T(2,128)(2,1)S(1)} %bitcast.128), channel_id=1, replica_groups=mesh['dp'=8,'tensor'=4] {'dp','tensor'}, dimensions={0}, use_global_device_ids=true | all-gather | bytes 8448 | tf_op jit(solution)/shard_map/all_gather | solution.py:82
  430.8 17.9 %all-gather.14.cloned.1.call-done = bf16[1024,1024]{1,0:T(8,128)(2,1)} async-done(((bf16[1024,128]{1,0:T(8,128)(2,1)}), bf16[1024,1024]{1,0:T(8,128)(2,1)}) %all-gather.14.cloned.1.call-update) | async-done | bytes 2097168 | tf_op jit(solution)/shard_map/all_gather | solution.py:34
  448.7 82.3 %all-gather.16.cloned.1.call-done = bf16[2048,1024]{1,0:T(8,128)(2,1)} async-done(((bf16[512,1024]{1,0:T(8,128)(2,1)}), bf16[2048,1024]{1,0:T(8,128)(2,1)}) %all-gather.16.cloned.1.call-update) | async-done | bytes 4194320 | tf_op jit(solution)/shard_map/all_gather | solution.py:177
  531.0 14.5 %convert_reduce_fusion = (f32[1024]{0:T(1024)}, bf16[2048,1024]{1,0:T(8,128)(2,1)S(1)}) fusion(f32[2048,1024]{1,0:T(8,128)} %fusion.73, f32[1024]{0:T(1024)S(1)} %dynamic_slice.37, bf16[2048,1024]{1,0:T(8,128)(2,1)} %all-gather.16.cloned.1.call-done, bf16[1024,1024]{1,0:T(8,128)(2,1)} %all-gather.14.cloned.1.call-done), kind=kOutput, calls=%fused_computation.60 | convolution fusion | flops 4343200768 | bytes 18882560 | tf_op jit(solution)/shard_map/rd,fd->rf/dot_general | solution.py:179
  566.8 62.6 %reduce-scatter.15.cloned.1.call-done = bf16[512,1024]{1,0:T(8,128)(2,1)} async-done(((bf16[2048,1024]{1,0:T(8,128)(2,1)}), bf16[512,1024]{1,0:T(8,128)(2,1)}) %reduce-scatter.15.cloned.1.call-update) | async-done | bytes 1048592 | tf_op jit(solution)/shard_map/reduce_scatter | solution.py:186
  635.4 73.5 %reduce-scatter.13.cloned.1.call-done = bf16[512,1024]{1,0:T(8,128)(2,1)} async-done(((bf16[2048,1024]{1,0:T(8,128)(2,1)}), bf16[512,1024]{1,0:T(8,128)(2,1)}) %reduce-scatter.13.cloned.1.call-update) | async-done | bytes 1048592 | tf_op jit(solution)/shard_map/reduce_scatter | solution.py:165
  715.6 81.2 %all-gather.18.cloned.1.call-done = bf16[2048,1024]{1,0:T(8,128)(2,1)} async-done(((bf16[512,1024]{1,0:T(8,128)(2,1)}), bf16[2048,1024]{1,0:T(8,128)(2,1)}) %all-gather.18.cloned.1.call-update) | async-done | bytes 4194320 | tf_op jit(solution)/shard_map/all_gather | solution.py:198
  802.3 222.9 %while.29 = (s32[]{:T(128)}, f32[2048,4,64]{0,2,1:T(8,128)S(1)}, f32[2048,4,64]{0,2,1:T(8,128)}, bf16[4,512,4,64]{1,3,2,0:T(8,128)(2,1)}, s32[4]{0:T(128)S(1)}, ...) while((s32[]{:T(128)}, f32[2048,4,64]{0,2,1:T(8,128)S(1)}, ...), condition=%wide.region_17.18_spmd.clone, body=%wide.region_15.17_spmd.clone.sunk | while | flops 2738616832 | bytes 216330608 | solution.py:238
  816.5 14.4 %multiply_reduce_fusion.3 = (f32[4,512]{1,0:T(4,128)S(1)}, f32[4,512,2048]{2,1,0:T(8,128)}) fusion(f32[4,512,2048]{2,1,0:T(8,128)} %fusion.157, f32[4,512]{1,0:T(4,128)S(1)} %dynamic-slice_bitcast_fusion.2, f32[512,2048]{1,0:T(8,128)S(1)} %subtract_convert_fusion.5, f32[4]{0:T(128)S(1)} %multiply_power_fusion.5, ...), kind=kOutput, calls=%fused_computation.23.clone.1 | convolution fusion | flops 566228992 | bytes 40124436 | tf_op jit(solution)/shard_map/while/body/eval_jaxpr/qhd,khd->hqk/dot_general | solution.py:42
  871.6 14.4 %multiply_reduce_fusion.3 = (f32[4,512]{1,0:T(4,128)S(1)}, f32[4,512,2048]{2,1,0:T(8,128)}) fusion(f32[4,512,2048]{2,1,0:T(8,128)} %fusion.157, f32[4,512]{1,0:T(4,128)S(1)} %dynamic-slice_bitcast_fusion.2, f32[512,2048]{1,0:T(8,128)S(1)} %subtract_convert_fusion.5, f32[4]{0:T(128)S(1)} %multiply_power_fusion.5, ...), kind=kOutput, calls=%fused_computation.23.clone.1 | convolution fusion | flops 566228992 | bytes 40124436 | tf_op jit(solution)/shard_map/while/body/eval_jaxpr/qhd,khd->hqk/dot_general | solution.py:42
  927.4 14.4 %multiply_reduce_fusion.3 = (f32[4,512]{1,0:T(4,128)S(1)}, f32[4,512,2048]{2,1,0:T(8,128)}) fusion(f32[4,512,2048]{2,1,0:T(8,128)} %fusion.157, f32[4,512]{1,0:T(4,128)S(1)} %dynamic-slice_bitcast_fusion.2, f32[512,2048]{1,0:T(8,128)S(1)} %subtract_convert_fusion.5, f32[4]{0:T(128)S(1)} %multiply_power_fusion.5, ...), kind=kOutput, calls=%fused_computation.23.clone.1 | convolution fusion | flops 566228992 | bytes 40124436 | tf_op jit(solution)/shard_map/while/body/eval_jaxpr/qhd,khd->hqk/dot_general | solution.py:42
  983.2 14.4 %multiply_reduce_fusion.3 = (f32[4,512]{1,0:T(4,128)S(1)}, f32[4,512,2048]{2,1,0:T(8,128)}) fusion(f32[4,512,2048]{2,1,0:T(8,128)} %fusion.157, f32[4,512]{1,0:T(4,128)S(1)} %dynamic-slice_bitcast_fusion.2, f32[512,2048]{1,0:T(8,128)S(1)} %subtract_convert_fusion.5, f32[4]{0:T(128)S(1)} %multiply_power_fusion.5, ...), kind=kOutput, calls=%fused_computation.23.clone.1 | convolution fusion | flops 566228992 | bytes 40124436 | tf_op jit(solution)/shard_map/while/body/eval_jaxpr/qhd,khd->hqk/dot_general | solution.py:42
  1035.2 13.1 fusion.70
  1081.2 28.7 %reduce-scatter.17.cloned.1.call-done = bf16[512,1024]{1,0:T(8,128)(2,1)} async-done(((bf16[2048,1024]{1,0:T(8,128)(2,1)}), bf16[512,1024]{1,0:T(8,128)(2,1)}) %reduce-scatter.17.cloned.1.call-update) | async-done | bytes 1048592 | tf_op jit(solution)/shard_map/reduce_scatter | solution.py:272
  1114.3 41.5 %all-reduce.17 = (f32[1024]{0:T(1024)S(1)}, f32[1024]{0:T(1024)S(1)}, f32[1024]{0:T(1024)S(1)}, f32[1024]{0:T(1024)S(1)}, f32[1024]{0:T(1024)S(1)}, /*index=5*/f...) all-reduce(f32[1024]{0:T(1024)S(1)} %get-tuple-element.199, ...), channel_id=6, replica_groups=mesh['dp'=8,'tensor'=4] {'dp','tensor'}, use_global_device_ids=true, to_apply=%region_22.23.clone | all-reduce | flops 12288 | bytes 98304
  1165.5 55.4 %reduce-scatter.27.cloned.1.call-done = f32[128,1024]{1,0:T(8,128)} async-done(((f32[1024,1024]{1,0:T(8,128)}), f32[128,1024]{1,0:T(8,128)}) %reduce-scatter.27.cloned.1.call-update) | async-done | bytes 524304 | tf_op jit(solution)/shard_map/reduce_scatter | solution.py:288
  1220.9 39.6 %reduce-scatter.25.cloned.1.call-done = f32[256,128]{1,0:T(8,128)} async-done(((f32[256,1024]{1,0:T(8,128)}), f32[256,128]{1,0:T(8,128)}) %reduce-scatter.25.cloned.1.call-update) | async-done | bytes 131088 | tf_op jit(solution)/shard_map/reduce_scatter | solution.py:291
  1260.5 39.7 %reduce-scatter.19.cloned.1.call-done = f32[128,256]{1,0:T(8,128)} async-done(((f32[1024,256]{1,0:T(8,128)}), f32[128,256]{1,0:T(8,128)}) %reduce-scatter.19.cloned.1.call-update) | async-done | bytes 131088 | tf_op jit(solution)/shard_map/reduce_scatter | solution.py:285
  1300.3 39.6 %reduce-scatter.21.cloned.1.call-done = f32[128,256]{1,0:T(8,128)} async-done(((f32[1024,256]{1,0:T(8,128)}), f32[128,256]{1,0:T(8,128)}) %reduce-scatter.21.cloned.1.call-update) | async-done | bytes 131088 | tf_op jit(solution)/shard_map/reduce_scatter | solution.py:286
  1339.9 39.7 %reduce-scatter.23.cloned.1.call-done = f32[128,256]{1,0:T(8,128)} async-done(((f32[1024,256]{1,0:T(8,128)}), f32[128,256]{1,0:T(8,128)}) %reduce-scatter.23.cloned.1.call-update) | async-done | bytes 131088 | tf_op jit(solution)/shard_map/reduce_scatter | solution.py:287
  (333 shorter events, 443.5 us)
Async XLA Ops:
  8.1 76.0 %copy-start.27 = (bf16[128,256]{1,0:T(8,128)(2,1)S(1)}, bf16[128,256]{1,0:T(8,128)(2,1)}, u32[]{:S(2)}) copy-start(bf16[128,256]{1,0:T(8,128)(2,1)} %param.27) | copy-start | bytes 196612
  8.1 85.9 %copy-start.28 = (bf16[256,128]{1,0:T(8,128)(2,1)S(1)}, bf16[256,128]{1,0:T(8,128)(2,1)}, u32[]{:S(2)}) copy-start(bf16[256,128]{1,0:T(8,128)(2,1)} %param.30) | copy-start | bytes 196612
  8.1 136.7 %all-gather.8.cloned.1.call-start = ((), (), s32[]{:S(2)}) async-start(), calls=%async_computation.10 | async-start | bytes 5242880 | tf_op jit(solution)/shard_map/all_gather | solution.py:118
  63.5 270.2 %reduce-scatter.11.cloned.1.call-start = ((), (), s32[]{:S(2)}) async-start(), calls=%async_computation.11 | async-start | bytes 5242880 | tf_op jit(solution)/shard_map/reduce_scatter | solution.py:150
  75.2 76.5 %copy-start.13 = (bf16[1024,256]{1,0:T(8,128)(2,1)}, bf16[1024,256]{1,0:T(8,128)(2,1)S(1)}, u32[]{:S(2)}) copy-start(bf16[1024,256]{1,0:T(8,128)(2,1)S(1)} %all_gather.66) | copy-start | bytes 1572868
  258.2 75.5 %copy-start.2 = (bf16[512,1024]{1,0:T(8,128)(2,1)S(1)}, bf16[512,1024]{1,0:T(8,128)(2,1)}, u32[]{:S(2)}) copy-start(bf16[512,1024]{1,0:T(8,128)(2,1)} %param.22) | copy-start | bytes 3145732
  258.2 149.9 %all-gather.12.cloned.1.call-start = ((), (), s32[]{:S(2)}) async-start(), calls=%async_computation.13 | async-start | bytes 2359296 | tf_op jit(solution)/shard_map/all_gather | solution.py:30
  258.8 161.4 %all-gather.10.cloned.1.call-start = ((), (), s32[]{:S(2)}) async-start(), calls=%async_computation.12 | async-start | bytes 5242880 | tf_op jit(solution)/shard_map/all_gather | solution.py:157
  338.8 109.9 %all-gather.14.cloned.1.call-start = ((), (), s32[]{:S(2)}) async-start(), calls=%async_computation.14 | async-start | bytes 2359296 | tf_op jit(solution)/shard_map/all_gather | solution.py:34
  339.4 191.6 %all-gather.16.cloned.1.call-start = ((), (), s32[]{:S(2)}) async-start(), calls=%async_computation.16 | async-start | bytes 5242880 | tf_op jit(solution)/shard_map/all_gather | solution.py:177
  340.1 289.3 %reduce-scatter.15.cloned.1.call-start = ((), (), s32[]{:S(2)}) async-start(), calls=%async_computation.17 | async-start | bytes 5242880 | tf_op jit(solution)/shard_map/reduce_scatter | solution.py:186
  408.1 146.3 %copy-start.38 = (f32[1024]{0:T(1024)}, f32[1024]{0:T(1024)S(1)}, u32[]{:S(2)}) copy-start(f32[1024]{0:T(1024)S(1)} %dynamic_slice.37) | copy-start | bytes 12292
  554.0 154.9 %reduce-scatter.13.cloned.1.call-start = ((), (), s32[]{:S(2)}) async-start(), calls=%async_computation.15 | async-start | bytes 5242880 | tf_op jit(solution)/shard_map/reduce_scatter | solution.py:165
  566.2 230.6 %all-gather.18.cloned.1.call-start = ((), (), s32[]{:S(2)}) async-start(), calls=%async_computation.18 | async-start | bytes 5242880 | tf_op jit(solution)/shard_map/all_gather | solution.py:198
  629.4 79.5 %copy-start.8 = (bf16[512,1024]{1,0:T(8,128)(2,1)S(1)}, bf16[512,1024]{1,0:T(8,128)(2,1)}, u32[]{:S(2)}) copy-start(bf16[512,1024]{1,0:T(8,128)(2,1)} %reduce-scatter.15.cloned.1.call-done) | copy-start | bytes 3145732
  713.0 83.7 %copy-start.20 = (bf16[256,1024]{1,0:T(8,128)(2,1)S(1)}, bf16[256,1024]{1,0:T(8,128)(2,1)}, u32[]{:S(2)}) copy-start(bf16[256,1024]{1,0:T(8,128)(2,1)} %all_gather.71) | copy-start | bytes 1572868
  715.5 394.4 %reduce-scatter.17.cloned.1.call-start = ((), (), s32[]{:S(2)}) async-start(), calls=%async_computation.19 | async-start | bytes 5242880 | tf_op jit(solution)/shard_map/reduce_scatter | solution.py:272
  1034.5 131.0 %reduce-scatter.29.cloned.1.call-start = ((), (), s32[]{:S(2)}) async-start(), calls=%async_computation.25 | async-start | bytes 4718592 | tf_op jit(solution)/shard_map/reduce_scatter | solution.py:292
  1048.3 172.6 %reduce-scatter.27.cloned.1.call-start = ((), (), s32[]{:S(2)}) async-start(), calls=%async_computation.24 | async-start | bytes 4718592 | tf_op jit(solution)/shard_map/reduce_scatter | solution.py:288
  1058.8 201.8 %reduce-scatter.25.cloned.1.call-start = ((), (), s32[]{:S(2)}) async-start(), calls=%async_computation.23 | async-start | bytes 1179648 | tf_op jit(solution)/shard_map/reduce_scatter | solution.py:291
  1064.4 235.8 %reduce-scatter.19.cloned.1.call-start = ((), (), s32[]{:S(2)}) async-start(), calls=%async_computation.20 | async-start | bytes 1179648 | tf_op jit(solution)/shard_map/reduce_scatter | solution.py:285
  1069.1 270.8 %reduce-scatter.21.cloned.1.call-start = ((), (), s32[]{:S(2)}) async-start(), calls=%async_computation.21 | async-start | bytes 1179648 | tf_op jit(solution)/shard_map/reduce_scatter | solution.py:286
  1073.7 305.9 %reduce-scatter.23.cloned.1.call-start = ((), (), s32[]{:S(2)}) async-start(), calls=%async_computation.22 | async-start | bytes 1179648 | tf_op jit(solution)/shard_map/reduce_scatter | solution.py:287
  1078.6 82.5 %copy-start.7 = (f32[512,1024]{1,0:T(8,128)S(1)}, f32[512,1024]{1,0:T(8,128)}, u32[]{:S(2)}) copy-start(f32[512,1024]{1,0:T(8,128)} %copy-done.6) | copy-start | bytes 6291460
  (47 other events, 931.5 us)
Sparse Core Ops, SparseCore 0:
  63.6 81.1 all-gather.7
  258.4 75.2 reduce-scatter.10
  554.1 75.2 reduce-scatter.14
  631.5 77.2 reduce-scatter.12
Sparse Core Ops, SparseCore 1:
  260.8 26.2 all-gather.11
  338.9 81.2 all-gather.9
  422.1 26.5 all-gather.13
  450.4 80.6 all-gather.15
  715.6 81.1 all-gather.17
  1034.6 75.3 reduce-scatter.16
  1113.7 51.8 reduce-scatter.28
  1169.7 51.2 reduce-scatter.26
  1224.6 35.9 reduce-scatter.24
  1264.3 35.9 reduce-scatter.18
  1303.9 35.9 reduce-scatter.20
  1343.6 35.9 reduce-scatter.22
where the time goes:
time: 1400 us; the launch traced here: 1390 us
  waiting for transfers between devices  691 us (49%)
  matrix products  313 us (22%)
  blocking collectives  192 us (14%)
  other arithmetic  112 us (8%)
  local copies, waits for them, and re-layouts  46.6 us (3%)
  between operations  16.2 us (1%)
  loops' own time  14.6 us (1%)
    dot_general x8, matrix products, block_scores(): jnp.einsum('qhd,khd->hqk', query_block, key_block, preferred_element_type...  86.2 us
    unnamed x2, blocking collectives  83.8 us
    all_gather x1, waiting for transfers between devices, per_device(): lax.all_gather(grad_output.astype(jnp.bfloat16), 'tensor', axis=0, tiled=...  82.3 us
    all_gather x1, waiting for transfers between devices, per_device(): lax.all_gather(grad_mixed.astype(jnp.bfloat16), 'tensor', axis=0, tiled=T...  81.2 us
    reduce_scatter x1, waiting for transfers between devices, per_device(): lax.psum_scatter(jnp.dot(attended, dense_full, preferred_element_type=jnp...  74.7 us
    reduce_scatter x1, waiting for transfers between devices, per_device(): lax.psum_scatter(jnp.dot(active, fc2_full, preferred_element_type=jnp.flo...  73.5 us
    all_gather x1, blocking collectives, per_device(): lax.all_gather(fc1_bias, ('dp', 'tensor'), axis=0, tiled=True)  67.9 us
    reduce_scatter x1, waiting for transfers between devices, per_device(): lax.psum_scatter(jnp.einsum('rf,df->rd', grad_pre, fc1_full, preferred_el...  62.6 us
  transfers between devices with their start and end apart: 16, of which 15 were waited for; matrix products, arithmetic and copies ran while one was open for 7% of the time, Pallas kernels for 0%

commit v1 on v0

v1 whole, which is shorter than its diff:
```python
import functools

import jax
import jax.numpy as jnp
from jax import lax
from jax.experimental import pallas as pl
from jax.experimental.pallas import tpu as pltpu
from jax.sharding import PartitionSpec as P

H = 16
HD = 64
MOST = 512
BLOCK = 256

EPSILON = 1e-05
EXCLUDED = 1e30
BF = jnp.bfloat16
F32 = jnp.float32


def norm_parts(values):
    center = jnp.mean(values, axis=-1, keepdims=True)
    centered = values - center
    spread = jnp.mean(centered * centered, axis=-1, keepdims=True)
    inverse = lax.rsqrt(spread + EPSILON)
    return centered * inverse, inverse


def norm_pull(grad, unit, inverse, gain):
    scaled = grad * gain
    mean_one = jnp.mean(scaled, axis=-1, keepdims=True)
    mean_two = jnp.mean(scaled * unit, axis=-1, keepdims=True)
    return inverse * (scaled - mean_one - unit * mean_two)


def gelu_tanh(values):
    return jax.nn.gelu(values, approximate=True)


def dot(left, right, left_dim=1, right_dim=0):
    return lax.dot_general(
        left, right, (((left_dim,), (right_dim,)), ((), ())), preferred_element_type=F32
    )


def slope_of(head):
    return jnp.exp2(-0.5 * (head.astype(F32) + 1.0))


def attend_kernel(q_ref, k_ref, v_ref, far_ref, o_ref, lse_ref):
    pair = pl.program_id(0)
    rows = q_ref.shape[0]
    window = BLOCK + MOST
    for place in range(2):
        slope = slope_of(jnp.full((1, 1), pair * 2 + place, jnp.int32))
        lanes = slice(place * HD, (place + 1) * HD)
        for block in range(rows // BLOCK):
            first = block * BLOCK
            mine = slice(first, first + BLOCK)
            keys = slice(first, first + window)
            scores = dot(q_ref[mine, lanes], k_ref[keys, lanes], 1, 1)
            scores = scores - slope * far_ref[mine, keys]
            highest = jnp.max(scores, axis=-1, keepdims=True)
            weights = jnp.exp(scores - highest)
            mass = jnp.sum(weights, axis=-1, keepdims=True)
            result = dot((weights * (1.0 / mass)).astype(BF), v_ref[keys, lanes])
            o_ref[mine, lanes] = result.astype(BF)
            lse_ref[place, mine, :] = highest + jnp.log(mass)


def attend_back_kernel(
    q_ref, k_ref, v_ref, far_ref, g_ref, lse_ref, dq_ref, dk_ref, dv_ref, dk_sum, dv_sum
):
    pair = pl.program_id(0)
    rows = q_ref.shape[0]
    window = BLOCK + MOST
    dk_sum[...] = jnp.zeros_like(dk_sum)
    dv_sum[...] = jnp.zeros_like(dv_sum)
    for place in range(2):
        slope = slope_of(jnp.full((1, 1), pair * 2 + place, jnp.int32))
        lanes = slice(place * HD, (place + 1) * HD)
        for block in range(rows // BLOCK):
            first = block * BLOCK
            mine = slice(first, first + BLOCK)
            keys = slice(first, first + window)
            query = q_ref[mine, lanes]
            key = k_ref[keys, lanes]
            grad = g_ref[mine, lanes]
            scores = dot(query, key, 1, 1) - slope * far_ref[mine, keys]
            probs = jnp.exp(scores - lse_ref[place, mine, :])
            grad_probs = dot(grad, v_ref[keys, lanes], 1, 1)
            weighted = jnp.sum(probs * grad_probs, axis=-1, keepdims=True)
            grad_scores = (probs * (grad_probs - weighted)).astype(BF)
            dq_ref[mine, lanes] = (dot(grad_scores, key) * HD ** (-0.5)).astype(BF)
            dk_sum[keys, lanes] += dot(grad_scores, query, 0, 0)
            dv_sum[keys, lanes] += dot(probs.astype(BF), grad, 0, 0)
    dk_ref[...] = dk_sum[...].astype(BF)
    dv_ref[...] = dv_sum[...].astype(BF)


def attend(query, keys, values, far):
    rows, width = query.shape
    reach = keys.shape[0]
    pairs = width // (2 * HD)
    column = pl.BlockSpec((rows, 2 * HD), lambda i: (0, i))
    tall = pl.BlockSpec((reach, 2 * HD), lambda i: (0, i))
    whole = pl.BlockSpec((rows, reach), lambda i: (0, 0))
    return pl.pallas_call(
        attend_kernel,
        grid=(pairs,),
        in_specs=[column, tall, tall, whole],
        out_specs=[column, pl.BlockSpec((2, rows, 1), lambda i: (i, 0, 0))],
        out_shape=[
            jax.ShapeDtypeStruct((rows, width), BF),
            jax.ShapeDtypeStruct((2 * pairs, rows, 1), F32),
        ],
        compiler_params=pltpu.CompilerParams(vmem_limit_bytes=40 * 1024 * 1024),
        cost_estimate=pl.CostEstimate(
            flops=40_000_000_000, bytes_accessed=20_000_000, transcendentals=6_000_000
        ),
    )(query, keys, values, far)


def attend_back(query, keys, values, far, grad, lse):
    rows, width = query.shape
    reach = keys.shape[0]
    pairs = width // (2 * HD)
    column = pl.BlockSpec((rows, 2 * HD), lambda i: (0, i))
    tall = pl.BlockSpec((reach, 2 * HD), lambda i: (0, i))
    whole = pl.BlockSpec((rows, reach), lambda i: (0, 0))
    mass = pl.BlockSpec((2, rows, 1), lambda i: (i, 0, 0))
    return pl.pallas_call(
        attend_back_kernel,
        grid=(pairs,),
        in_specs=[column, tall, tall, whole, column, mass],
        out_specs=[column, tall, tall],
        out_shape=[
            jax.ShapeDtypeStruct((rows, width), BF),
            jax.ShapeDtypeStruct((reach, width), BF),
            jax.ShapeDtypeStruct((reach, width), BF),
        ],
        scratch_shapes=[pltpu.VMEM((reach, 2 * HD), F32), pltpu.VMEM((reach, 2 * HD), F32)],
        compiler_params=pltpu.CompilerParams(vmem_limit_bytes=40 * 1024 * 1024),
        cost_estimate=pl.CostEstimate(
            flops=80_000_000_000, bytes_accessed=30_000_000, transcendentals=6_000_000
        ),
    )(query, keys, values, far, grad, lse)


def gather_plane(parts):
    count = len(parts)
    rows, width = parts[0].shape
    packed = jnp.concatenate(parts, axis=1)
    lines = lax.all_gather(packed, "tensor", axis=0, tiled=False)
    tensor = lines.shape[0]
    lines = lines.reshape(tensor, rows, count, width).transpose(1, 2, 0, 3)
    lines = lines.reshape(rows, count * tensor * width)
    return lax.all_gather(lines, "dp", axis=0, tiled=True)


def scatter_line(summed, count):
    rows = summed.shape[0]
    tensor = lax.axis_size("tensor")
    split = summed.reshape(rows, count, tensor, -1).transpose(2, 0, 1, 3)
    own = lax.psum_scatter(split, "tensor", scatter_dimension=0, tiled=False)
    return [own[:, i, :].astype(F32) for i in range(count)]


def scatter_plane(grads):
    return lax.psum_scatter(grads, "dp", scatter_dimension=0, tiled=True)


def per_device(
    block_input,
    ln1_gain,
    ln1_bias,
    w_query,
    w_key,
    w_value,
    query_bias,
    value_bias,
    w_dense,
    dense_bias,
    ln2_gain,
    ln2_bias,
    w_fc1,
    fc1_bias,
    w_fc2,
    fc2_bias,
    out_grad,
    doc_lengths,
):
    rows, width = block_input.shape
    dp = lax.axis_size("dp")
    tensor = lax.axis_size("tensor")
    place = lax.axis_index("tensor")
    onward = [(i, i + 1) for i in range(tensor - 1)]
    backward = [(i + 1, i) for i in range(tensor - 1)]

    halo = lax.ppermute(block_input, "tensor", onward)

    small = jnp.concatenate(
        [
            ln1_gain,
            ln1_bias,
            query_bias,
            value_bias,
            dense_bias,
            ln2_gain,
            ln2_bias,
            fc1_bias,
            fc2_bias,
        ]
    )
    small_width = small.shape[0]
    piece = ln1_gain.shape[0]
    hidden_piece = fc1_bias.shape[0]
    padded = -(-small_width // 128) * 128
    small = jnp.pad(small, (0, padded - small_width))[None]
    vectors = lax.all_gather(small, ("dp", "tensor"), axis=0, tiled=True).astype(F32)
    pieces = [piece] * 7 + [hidden_piece, piece]
    starts = [sum(pieces[:i]) for i in range(len(pieces))]
    (
        gain_first,
        shift_first,
        query_shift,
        value_shift,
        dense_shift,
        gain_second,
        shift_second,
        hidden_shift,
        output_shift,
    ) = [vectors[:, s : s + n].reshape(-1) for s, n in zip(starts, pieces)]

    attn_weights = gather_plane([w_query, w_key, w_value, w_dense.T])
    ffn_first = gather_plane([w_fc1])
    ffn_second = gather_plane([w_fc2.T])
    qkv_weights = attn_weights[:, : 3 * width]
    dense_t = attn_weights[:, 3 * width :]

    extended = jnp.concatenate([halo, block_input], axis=0).astype(F32)
    unit_first, inverse_first = norm_parts(extended)
    normed_in = (unit_first * gain_first + shift_first).astype(BF)
    qkv_shift = jnp.concatenate([query_shift, jnp.zeros_like(query_shift), value_shift])
    query = (
        (dot(normed_in[rows:], qkv_weights[:, :width]) + query_shift).astype(BF) * HD ** (-0.5)
    ).astype(BF)
    kv = (dot(normed_in, qkv_weights[:, width:]) + qkv_shift[width:]).astype(BF)
    keys, values = kv[:, :width], kv[:, width:]

    doc_ends = jnp.cumsum(doc_lengths[0])
    key_rows = place * rows - rows + jnp.arange(2 * rows, dtype=jnp.int32)
    segment = jnp.sum((key_rows[:, None] >= doc_ends[None, :]).astype(jnp.int32), axis=1)
    segment = jnp.where(key_rows < 0, -1, segment)
    query_rows = key_rows[rows:]
    distance = query_rows[:, None] - key_rows[None, :]
    allowed = (distance >= 0) & (segment[rows:, None] == segment[None, :])
    far = jnp.where(allowed, distance.astype(F32), EXCLUDED)

    attended, lse = attend(query, keys, values, far)

    rows_in = block_input.astype(F32)
    mixed = rows_in + dot(attended, dense_t, 1, 1) + dense_shift
    unit_second, inverse_second = norm_parts(mixed)
    normed_mid = (unit_second * gain_second + shift_second).astype(BF)
    pre_act = dot(normed_mid, ffn_first) + hidden_shift
    active, gelu_pull = jax.vjp(gelu_tanh, pre_act)
    active = active.astype(BF)
    block_output = (mixed + dot(active, ffn_second, 1, 1) + output_shift).astype(BF)

    grad_output = out_grad.astype(F32)
    grad_fc2 = dot(out_grad, active, 0, 0).astype(BF)
    fc2_sum = scatter_plane(grad_fc2)
    grad_active = dot(out_grad, ffn_second)
    grad_pre = gelu_pull(grad_active)[0].astype(BF)
    grad_fc1 = dot(normed_mid, grad_pre, 0, 0).astype(BF)
    fc1_sum = scatter_plane(grad_fc1)
    grad_mid = dot(grad_pre, ffn_first, 1, 1)
    grad_mixed = grad_output + norm_pull(grad_mid, unit_second, inverse_second, gain_second)
    grad_attn = grad_mixed.astype(BF)
    grad_dense = dot(grad_attn, attended, 0, 0).astype(BF)
    grad_attended = dot(grad_attn, dense_t).astype(BF)

    grad_query, grad_keys, grad_values = attend_back(query, keys, values, far, grad_attended, lse)
    grad_kv = jnp.concatenate([grad_keys, grad_values], axis=1)
    grad_in_kv = dot(grad_kv, qkv_weights[:, width:], 1, 1)
    grad_in_own = grad_in_kv[rows:] + dot(grad_query, qkv_weights[:, :width], 1, 1)
    grad_in_halo = grad_in_kv[:rows]
    returned = lax.ppermute(grad_in_halo.astype(BF), "tensor", backward)

    own_unit = unit_first[rows:]
    halo_unit = unit_first[:rows]
    small_grads = [
        jnp.sum(grad_in_own * own_unit, axis=0) + jnp.sum(grad_in_halo * halo_unit, axis=0),
        jnp.sum(grad_in_own, axis=0) + jnp.sum(grad_in_halo, axis=0),
        jnp.sum(grad_query.astype(F32), axis=0),
        jnp.sum(grad_values.astype(F32), axis=0),
        jnp.sum(grad_mixed, axis=0),
        jnp.sum(grad_mid * unit_second, axis=0),
        jnp.sum(grad_mid, axis=0),
        jnp.sum(grad_pre.astype(F32), axis=0),
        jnp.sum(grad_output, axis=0),
    ]
    shares = [g.reshape(dp, tensor, -1) for g in small_grads]
    shares = jnp.concatenate(shares, axis=2)
    shares = jnp.pad(shares, ((0, 0), (0, 0), (0, padded - small_width)))
    block_width = width // dp
    lanes = 128 * -(-(tensor * padded) // (128 * block_width))
    shares = shares.reshape(dp, tensor * padded)
    shares = jnp.pad(shares, ((0, 0), (0, block_width * lanes - tensor * padded)))
    shares = shares.reshape(width, lanes).astype(BF)

    grad_q_w = dot(normed_in[rows:], grad_query, 0, 0).astype(BF)
    grad_kv_w = dot(normed_in, grad_kv, 0, 0).astype(BF)
    last_sum = scatter_plane(jnp.concatenate([grad_q_w, grad_kv_w, grad_dense, shares], axis=1))

    grad_normed = grad_in_own + returned.astype(F32)
    input_grad = grad_mixed + norm_pull(grad_normed, own_unit, inverse_first[rows:], gain_first)

    (fc2_own,) = scatter_line(fc2_sum, 1)
    (fc1_own,) = scatter_line(fc1_sum, 1)
    split = last_sum[:, : 4 * width].reshape(block_width, 4, tensor, -1).transpose(2, 0, 1, 3)
    split = split.reshape(tensor, block_width, -1)
    small_sum = last_sum[:, 4 * width :].reshape(-1)[: tensor * padded].reshape(tensor, padded)
    extra = split.shape[2]
    small_rows = -(-padded // extra)
    small_sum = jnp.pad(small_sum, ((0, 0), (0, small_rows * extra - padded)))
    split = jnp.concatenate([split, small_sum.reshape(tensor, small_rows, extra)], axis=1)
    own = lax.psum_scatter(split, "tensor", scatter_dimension=0, tiled=False)
    own_small = own[block_width:].reshape(-1).astype(F32)
    own = own[:block_width].reshape(block_width, 4, -1).astype(F32)
    out_small = [own_small[s : s + n] for s, n in zip(starts, pieces)]
    return (
        block_output,
        input_grad,
        out_small[0],
        out_small[1],
        own[:, 0],
        own[:, 1],
        own[:, 2],
        out_small[2],
        out_small[3],
        own[:, 3].T,
        out_small[4],
        out_small[5],
        out_small[6],
        fc1_own,
        out_small[7],
        fc2_own.T,
        out_small[8],
    )


def solution(mesh):
    every = P(("dp", "tensor"))
    tokens = P(("dp", "tensor"), None)
    row_cut = P("dp", "tensor")
    col_cut = P("tensor", "dp")
    return jax.shard_map(
        per_device,
        mesh=mesh,
        in_specs=(
            tokens,
            every,
            every,
            row_cut,
            row_cut,
            row_cut,
            every,
            every,
            col_cut,
            every,
            every,
            every,
            row_cut,
            every,
            col_cut,
            every,
            tokens,
            P("dp", None),
        ),
        out_specs=(
            tokens,
            tokens,
            every,
            every,
            row_cut,
            row_cut,
            row_cut,
            every,
            every,
            col_cut,
            every,
            every,
            every,
            row_cut,
            every,
            col_cut,
            every,
        ),
        check_vma=False,
    )
```

time: 1400 us -> 646 us (0.46)
  waiting for transfers between devices: 691 us -> 279 us
  matrix products: 313 us -> 110 us
  blocking collectives: 192 us -> 83.8 us
  other arithmetic: 112 us -> 32.7 us
  Pallas kernels: 0 us -> 55.7 us
  loops' own time: 14.6 us -> 0 us
    reduce_scatter x10 -> x5, waiting for transfers between devices: 455 us -> 147 us  [the longest x2 73.5 us: scatter_plane(): return lax.psum_scatter(grads, 'dp', scatter_dimension=0, tiled=True)]
    dot_general x46 -> x15, matrix products: 313 us -> 110 us  [dot(): lax.dot_general(left, right, (((left_dim,), (right_dim,)), ((), ())), pre...]
    all_gather x6, waiting for transfers between devices: 234 us -> 107 us  [the longest x3 82.8 us: gather_plane(): lines = lax.all_gather(packed, 'tensor', axis=0, tiled=False)]
    unnamed x2 -> x0, blocking collectives: 83.8 us -> none
    pallas_call x0 -> x2, Pallas kernels: none -> 55.7 us  [the longest x1 34.7 us: attend_back(): pl.pallas_call(attend_back_kernel, grid=(pairs,), in_specs=[column, tall,...]
    convert_element_type x23 -> x3, other arithmetic: 54.1 us -> 2.82 us  [the longest x1 1.79 us: scatter_line(): return [own[:, i, :].astype(F32) for i in range(count)]]
    reduce_sum x16 -> x8, other arithmetic: 46.2 us -> 8.03 us  [the longest x1 3.03 us: per_device(): jnp.sum(grad_mixed, axis=0)]
    all_gather x5 -> x1, blocking collectives: 108 us -> 83.8 us  [per_device(): lax.all_gather(small, ('dp', 'tensor'), axis=0, tiled=True).astype(F32)]
  transfers between devices with their start and end apart: 16 -> 14, of which waited for: 15 -> 10; matrix products, arithmetic and copies ran while one was open for 7% -> 25% of each run, Pallas kernels for 0% -> 9%
where the time goes in v1:
time: 646 us; the launch traced here: 638 us
  waiting for transfers between devices  279 us (43%)
  matrix products  110 us (17%)
  blocking collectives  83.8 us (13%)
  Pallas kernels  55.7 us (9%)
  local copies, waits for them, and re-layouts  53.7 us (8%)
  other arithmetic  32.7 us (5%)
  between operations  15.4 us (2%)
  starting transfers between devices  7.03 us (1%)
    dot_general x15, matrix products, dot(): lax.dot_general(left, right, (((left_dim,), (right_dim,)), ((), ())), pre...  110 us
    all_gather x1, blocking collectives, per_device(): lax.all_gather(small, ('dp', 'tensor'), axis=0, tiled=True).astype(F32)  83.8 us
    all_gather x3, waiting for transfers between devices, gather_plane(): lines = lax.all_gather(packed, 'tensor', axis=0, tiled=False)  82.8 us
    reduce_scatter x2, waiting for transfers between devices, scatter_plane(): return lax.psum_scatter(grads, 'dp', scatter_dimension=0, tiled=True)  73.5 us
    reduce_scatter x1, waiting for transfers between devices, per_device(): own = lax.psum_scatter(split, 'tensor', scatter_dimension=0, tiled=False)  43 us
    pallas_call x1, Pallas kernels, attend_back(): pl.pallas_call(attend_back_kernel, grid=(pairs,), in_specs=[column, tall,...  34.7 us
    reduce_scatter x2, waiting for transfers between devices, scatter_line(): own = lax.psum_scatter(split, 'tensor', scatter_dimension=0, tiled=False)  30.8 us
    unnamed x98, local copies, waits for them, and re-layouts  25.3 us
  transfers between devices with their start and end apart: 14, of which 10 were waited for; matrix products, arithmetic and copies ran while one was open for 25% of the time, Pallas kernels for 9%

profile of v1, /device:TPU:0, one launch (start us, length us, event | category | flops | bytes accessed | tf_op | source)
XLA Modules:
  0.0 637.9 jit_solution(559429738335613539)
XLA Ops:
  14.4 30.4 %all-gather.18.cloned.1.call-done = bf16[512,1024]{0,1:T(8,128)(2,1)} async-done(((bf16[128,1024]{0,1:T(8,128)(2,1)}), bf16[512,1024]{0,1:T(8,128)(2,1)}) %all-gather.18.cloned.1.call-update) | async-done | bytes 1048592 | tf_op jit(solution)/shard_map/all_gather | solution.py:154
  47.4 25.2 %all-gather.20.cloned.1.call-done = bf16[512,1024]{1,0:T(8,128)(2,1)} async-done(((bf16[128,1024]{1,0:T(8,128)(2,1)}), bf16[512,1024]{1,0:T(8,128)(2,1)}) %all-gather.20.cloned.1.call-update) | async-done | bytes 1048592 | tf_op jit(solution)/shard_map/all_gather | solution.py:154
  75.0 27.2 %all-gather.22.cloned.1.call-done = bf16[512,1024]{1,0:T(8,128)(2,1)} async-done(((bf16[128,1024]{1,0:T(8,128)(2,1)}), bf16[512,1024]{1,0:T(8,128)(2,1)}) %all-gather.22.cloned.1.call-update) | async-done | bytes 1048592 | tf_op jit(solution)/shard_map/all_gather | solution.py:154
  109.1 83.8 %all-gather.4 = bf16[32,1,384]{2,1,0:T(2,128)(2,1)S(1)} all-gather(bf16[1,1,384]{2,1,0:T(2,128)(2,1)S(1)} %reshape.280), channel_id=2, replica_groups=mesh['dp'=8,'tensor'=4] {'dp','tensor'}, dimensions={0}, use_global_device_ids=true | all-gather | bytes 25344 | tf_op jit(solution)/shard_map/all_gather | solution.py:220
  199.1 4.8 fusion.7
  203.9 7.6 %add_convert_fusion = bf16[1024,2048]{1,0:T(8,128)(2,1)S(1)} fusion(f32[2048]{0:T(1024)S(1)} %concatenate.28, bf16[1024,1024]{1,0:T(8,128)(2,1)} %get-tuple-element.71, bf16[1024,4096]{0,1:T(8,128)(2,1)} %all-gather.12.cloned.1.call-done), kind=kOutput, calls=%fused_computation.12 | convolution fusion | flops 4299161600 | bytes 10493952 | tf_op jit(solution)/shard_map/dot_general | solution.py:41
  214.4 21.0 %shard_map.305 = (bf16[512,1024]{1,0:T(8,128)(2,1)S(1)}, f32[16,512,1]{2,1,0:T(8,128)S(1)}) custom-call(bf16[512,1024]{1,0:T(8,128)(2,1)S(1)} %fusion.33.q_ref, bf16[1024,1024]{1,0:T(8,128)(2,1)S(1)} %get-tuple-element.69.k_ref, bf16[1024,1024]{1,0:T(8,128)(2,1)S(1)} %get-tuple-element.68.v_ref, f32[512,1024]{1,0:T(8,128)S(1)} %fusion.13.far_ref), custom_call_target="tpu_custom_call" | custom-call | flops 40000000000 | bytes 20000000 | tf_op jit(solution)/shard_map/pallas_call | solution.py:108
  239.4 11.9 %fusion.41 = f32[512,4096]{1,0:T(8,128)} fusion(bf16[1024,4096]{0,1:T(8,128)(2,1)} %all-gather.14.cloned.1.call-done, f32[512,1024]{1,0:T(8,128)} %copy-done.12, f32[1024]{0:T(1024)S(1)} %add.188, f32[1024]{0:T(1024)S(1)} %mul.166, f32[512]{0:T(512)S(1)} %add_rsqrt_fusion.1, f32[512]{0:T(512)S(1)} %broadcast_multiply_fusion.5), kind=kOutput, calls=%fused_computation.99 | convolution fusion | flops 4297588736 | bytes 18886656 | tf_op jit(solution)/shard_map/dot_general | solution.py:41
  251.4 24.2 %all-gather.16.cloned.1.call-done = bf16[1024,4096]{0,1:T(8,128)(2,1)} async-done(((bf16[128,4096]{0,1:T(8,128)(2,1)}), bf16[1024,4096]{0,1:T(8,128)(2,1)}) %all-gather.16.cloned.1.call-update) | async-done | bytes 8388624 | tf_op jit(solution)/shard_map/all_gather | solution.py:158
  275.6 13.8 %fusion.42 = (bf16[4096]{0:T(1024)(128)(2,1)}, bf16[512,4096]{1,0:T(8,128)(2,1)S(1)}) fusion(f32[512,4096]{1,0:T(8,128)} %fusion.41, f32[4096]{0:T(1024)S(1)} %slice_bitcast_fusion.1, bf16[512,1024]{1,0:T(8,128)(2,1)S(1)} %copy-done.17, bf16[1024,4096]{0,1:T(8,128)(2,1)} %all-gather.16.cloned.1.call-done), kind=kOutput, calls=%fused_computation.100 | convolution fusion | flops 4341100544 | bytes 22044672 | tf_op jit(solution)/shard_map/dot_general | solution.py:41
  291.4 7.7 %convolution_convert_fusion = bf16[1024,4096]{1,0:T(8,128)(2,1)} fusion(bf16[512,4096]{1,0:T(8,128)(2,1)S(1)} %get-tuple-element.65, f32[512,1024]{1,0:T(8,128)S(1)} %copy-done.13, f32[1024]{0:T(1024)S(1)} %add.188, f32[1024]{0:T(1024)S(1)} %mul.166, f32[512]{0:T(512)S(1)} %add_rsqrt_fusion.1, f32[512]{0:T(512)S(1)} %broadcast_multiply_fusion.5), kind=kOutput, calls=%fused_computation.13 | convolution fusion | flops 4301783040 | bytes 14692352 | tf_op jit(solution)/shard_map/dot_general | solution.py:41
  299.4 14.3 %convert_bitcast_fusion = bf16[1024,4096]{0,1:T(8,128)(2,1)} fusion(bf16[512,1024]{1,0:T(8,128)(2,1)S(1)} %copy-done.17, f32[512,4096]{1,0:T(8,128)} %fusion.41, f32[4096]{0:T(1024)S(1)} %slice_bitcast_fusion.1), kind=kOutput, calls=%fused_computation.10 | convolution fusion | flops 4320133120 | bytes 17842176 | tf_op jit(solution)/shard_map/dot_general | solution.py:41
  313.7 11.9 %copy.125 = bf16[1024,4096]{1,0:T(8,128)(2,1)} copy(bf16[1024,4096]{0,1:T(8,128)(2,1)} %convert_bitcast_fusion) | data formatting | bytes 16777216
  325.5 11.3 %multiply_reduce_fusion = (bf16[1024]{0:T(1024)(128)(2,1)S(1)}, f32[512]{0:T(512)S(1)}, f32[512]{0:T(512)S(1)}, bf16[1024]{0:T(1024)(128)(2,1)S(1)}, f32[512,1024]{1,0:T(8,128)}) fusion(f32[512,1024]{1,0:T(8,128)} %copy-done.12, f32[512]{0:T(512)S(1)} %add_rsqrt_fusion.1, f32[512]{0:T(512)S(1)} %broadcast_multiply_fusion.5, f32[1024]{0:T(1024)S(1)} %mul.166, ...), kind=kOutput, calls=%fused_computation.32 | convolution fusion | flops 4299682816 | bytes 16793600 | tf_op jit(solution)/shard_map/dot_general | solution.py:41
  344.1 34.7 %shard_map.306 = (bf16[512,1024]{1,0:T(8,128)(2,1)S(1)}, bf16[1024,1024]{1,0:T(8,128)(2,1)S(1)}, bf16[1024,1024]{1,0:T(8,128)(2,1)S(1)}) custom-call(bf16[512,1024]{1,0:T(8,128)(2,1)S(1)} %copy-done.7, bf16[1024,1024]{1,0:T(8,128)(2,1)S(1)} %copy-done.3, bf16[1024,1024]{1,0:T(8,128)(2,1)S(1)} %copy-done.1, f32[512,1024]{1,0:T(8,128)S(1)} %fusion.13.far_ref, ...), custom_call_target="tpu_custom_call" | custom-call | flops 80000000000 | bytes 30000000 | tf_op jit(solution)/shard_map/pallas_call | solution.py:132
  396.1 9.6 %convolution_convert_fusion.1 = bf16[1024,2048]{1,0:T(8,128)(2,1)} fusion(bf16[1024,1024]{1,0:T(8,128)(2,1)} %get-tuple-element.71, bf16[1024,2048]{1,0:T(8,128)(2,1)} %copy-done.21), kind=kOutput, calls=%fused_computation.20 | convolution fusion | flops 4297064448 | bytes 10485760 | tf_op jit(solution)/shard_map/dot_general | solution.py:41
  405.7 8.4 %collective-permute-done.1 = bf16[512,1024]{1,0:T(8,128)(2,1)} collective-permute-done((bf16[512,1024]{1,0:T(8,128)(2,1)}, bf16[512,1024]{1,0:T(8,128)(2,1)}, u32[]{:S(2)}, u32[]{:S(2)}) %collective-permute-start.1) | collective-permute-done | bytes 1048608 | tf_op jit(solution)/shard_map/ppermute | solution.py:289
  414.1 5.5 slice_reduce_fusion
  420.1 6.5 %pad_maximum_fusion = bf16[1024,4224]{1,0:T(8,128)(2,1)} fusion(bf16[1024,128]{1,0:T(8,128)(2,1)S(1)} %convert_element_type.129, bf16[1024,1024]{1,0:T(8,128)(2,1)} %convolution_convert_fusion.2, bf16[1024,2048]{1,0:T(8,128)(2,1)} %convolution_convert_fusion.1, bf16[1024,1024]{1,0:T(8,128)(2,1)S(1)} %copy.114), kind=kLoop, calls=%fused_computation.2 | loop fusion | flops 34603008 | bytes 17301504 | tf_op jit(solution)/shard_map/concatenate | solution.py:315
  430.1 15.6 %reduce-scatter.19.cloned.1.call-done = bf16[128,4096]{1,0:T(8,128)(2,1)} async-done(((bf16[1024,4096]{1,0:T(8,128)(2,1)}), bf16[128,4096]{1,0:T(8,128)(2,1)}) %reduce-scatter.19.cloned.1.call-update) | async-done | bytes 1048592
  448.4 73.5 %reduce-scatter.9.cloned.1.call-done = bf16[128,4224]{1,0:T(8,128)(2,1)} async-done(((bf16[1024,4224]{1,0:T(8,128)(2,1)}), bf16[128,4224]{1,0:T(8,128)(2,1)}) %reduce-scatter.9.cloned.1.call-update) | async-done | bytes 1081360 | tf_op jit(solution)/shard_map/reduce_scatter | solution.py:170
  531.2 12.4 %add_convert_fusion.2 = bf16[512,1024]{1,0:T(8,128)(2,1)} fusion(f32[512,1024]{1,0:T(8,128)S(1)} %copy-done.14, bf16[1024,4096]{0,1:T(8,128)(2,1)} %all-gather.16.cloned.1.call-done, f32[1024]{0:T(1024)S(1)} %add.197, f32[512,4096]{1,0:T(8,128)} %fusion.41, f32[4096]{0:T(1024)S(1)} %slice_bitcast_fusion.1), kind=kOutput, calls=%fused_computation.39 | convolution fusion | flops 4317511680 | bytes 19943424 | tf_op jit(solution)/shard_map/dot_general | solution.py:41
  553.1 26.3 %reduce-scatter.17.cloned.1.call-done = bf16[1,128,1,1024]{1,3,2,0:T(8,128)(2,1)} async-done(((bf16[4,128,1,1024]{1,3,2,0:T(8,128)(2,1)}), bf16[1,128,1,1024]{1,3,2,0:T(8,128)(2,1)}) %reduce-scatter.17.cloned.1.call-update) | async-done | bytes 262160 | tf_op jit(solution)/shard_map/reduce_scatter | solution.py:165
  581.2 43.0 %reduce-scatter.11.cloned.1.call-done = bf16[1,129,1024]{1,2,0:T(8,128)(2,1)} async-done(((bf16[4,129,1024]{1,2,0:T(8,128)(2,1)}), bf16[1,129,1024]{1,2,0:T(8,128)(2,1)}) %reduce-scatter.11.cloned.1.call-update) | async-done | bytes 264208 | tf_op jit(solution)/shard_map/reduce_scatter | solution.py:329
  (213 shorter events, 91.9 us)
Async XLA Ops:
  7.2 37.6 %all-gather.18.cloned.1.call-start = ((), (), s32[]{:S(2)}) async-start(), calls=%async_computation.14 | async-start | bytes 1310720 | tf_op jit(solution)/shard_map/all_gather | solution.py:154
  11.7 60.9 %all-gather.20.cloned.1.call-start = ((), (), s32[]{:S(2)}) async-start(), calls=%async_computation.15 | async-start | bytes 1310720 | tf_op jit(solution)/shard_map/all_gather | solution.py:154
  12.5 89.7 %all-gather.22.cloned.1.call-start = ((), (), s32[]{:S(2)}) async-start(), calls=%async_computation.16 | async-start | bytes 1310720 | tf_op jit(solution)/shard_map/all_gather | solution.py:154
  14.3 189.6 %all-gather.12.cloned.1.call-start = ((), (), s32[]{:S(2)}) async-start(), calls=%async_computation.6 | async-start | bytes 9437184 | tf_op jit(solution)/shard_map/all_gather | solution.py:158
  47.3 61.7 %copy-start.30 = (bf16[32]{0:T(256)(128)(2,1)S(1)}, bf16[32]{0:T(256)(128)(2,1)}, u32[]{:S(2)}) copy-start(bf16[32]{0:T(256)(128)(2,1)} %param.19) | copy-start | bytes 196
  47.3 61.7 %copy-start.31 = (bf16[32]{0:T(256)(128)(2,1)S(1)}, bf16[32]{0:T(256)(128)(2,1)}, u32[]{:S(2)}) copy-start(bf16[32]{0:T(256)(128)(2,1)} %param.20) | copy-start | bytes 196
  47.3 61.7 %copy-start.32 = (bf16[32]{0:T(256)(128)(2,1)S(1)}, bf16[32]{0:T(256)(128)(2,1)}, u32[]{:S(2)}) copy-start(bf16[32]{0:T(256)(128)(2,1)} %param.24) | copy-start | bytes 196
  47.3 61.7 %copy-start.33 = (bf16[32]{0:T(256)(128)(2,1)S(1)}, bf16[32]{0:T(256)(128)(2,1)}, u32[]{:S(2)}) copy-start(bf16[32]{0:T(256)(128)(2,1)} %param.25) | copy-start | bytes 196
  47.3 61.6 %copy-start.34 = (bf16[32]{0:T(256)(128)(2,1)S(1)}, bf16[32]{0:T(256)(128)(2,1)}, u32[]{:S(2)}) copy-start(bf16[32]{0:T(256)(128)(2,1)} %param.27) | copy-start | bytes 196
  47.3 61.6 %copy-start.35 = (bf16[32]{0:T(256)(128)(2,1)S(1)}, bf16[32]{0:T(256)(128)(2,1)}, u32[]{:S(2)}) copy-start(bf16[32]{0:T(256)(128)(2,1)} %param.28) | copy-start | bytes 196
  47.3 61.6 %copy-start.36 = (bf16[32]{0:T(256)(128)(2,1)S(1)}, bf16[32]{0:T(256)(128)(2,1)}, u32[]{:S(2)}) copy-start(bf16[32]{0:T(256)(128)(2,1)} %param.29) | copy-start | bytes 196
  47.3 61.6 %copy-start.37 = (bf16[128]{0:T(256)(128)(2,1)S(1)}, bf16[128]{0:T(256)(128)(2,1)}, u32[]{:S(2)}) copy-start(bf16[128]{0:T(256)(128)(2,1)} %param.31) | copy-start | bytes 772
  47.3 61.6 %copy-start.38 = (bf16[32]{0:T(256)(128)(2,1)S(1)}, bf16[32]{0:T(256)(128)(2,1)}, u32[]{:S(2)}) copy-start(bf16[32]{0:T(256)(128)(2,1)} %param.33) | copy-start | bytes 196
  47.3 146.6 %copy-start.40 = (s32[1,8]{1,0:T(1,128)S(1)}, s32[1,8]{1,0:T(1,128)}, u32[]{:S(2)}) copy-start(s32[1,8]{1,0:T(1,128)} %param.35) | copy-start | bytes 100
  47.4 192.1 %all-gather.14.cloned.1.call-start = ((), (), s32[]{:S(2)}) async-start(), calls=%async_computation.7 | async-start | bytes 9437184 | tf_op jit(solution)/shard_map/all_gather | solution.py:158
  74.9 200.7 %all-gather.16.cloned.1.call-start = ((), (), s32[]{:S(2)}) async-start(), calls=%async_computation.8 | async-start | bytes 9437184 | tf_op jit(solution)/shard_map/all_gather | solution.py:158
  104.5 322.3 %reduce-scatter.13.cloned.1.call-start = ((), (), s32[]{:S(2)}) async-start(), calls=%async_computation.11 | async-start | bytes 9437184 | tf_op jit(solution)/shard_map/reduce_scatter | solution.py:170
  104.6 90.5 %collective-permute-start = (bf16[512,1024]{1,0:T(8,128)(2,1)S(1)}, bf16[512,1024]{1,0:T(8,128)(2,1)}, u32[]{:S(2)}, u32[]{:S(2)}) collective-permute-start(bf16[512,1024]{1,0:T(8,128)(2,1)S(1)} %copy-done.11), channel_id=1, source_target_pairs={{0,1},{1,2},{2,3},{4,5},{5,6},{6,7},{8,9},{9,10},{10,11},{12,13},{... | collective-permute-start | bytes 3145736 | tf_op jit(solution)/shard_map/ppermute | solution.py:200
  299.1 146.6 %reduce-scatter.19.cloned.1.call-start = ((), (), s32[]{:S(2)}) async-start(), calls=%async_computation.17 | async-start | bytes 9437184
  336.8 185.1 %reduce-scatter.9.cloned.1.call-start = ((), (), s32[]{:S(2)}) async-start(), calls=%async_computation.9 | async-start | bytes 9732096 | tf_op jit(solution)/shard_map/reduce_scatter | solution.py:170
  385.6 28.6 %collective-permute-start.1 = (bf16[512,1024]{1,0:T(8,128)(2,1)}, bf16[512,1024]{1,0:T(8,128)(2,1)}, u32[]{:S(2)}, u32[]{:S(2)}) collective-permute-start(bf16[512,1024]{1,0:T(8,128)(2,1)} %slice.288), channel_id=1, source_target_pairs={{1,0},{2,1},{3,2},{5,4},{6,5},{7,6},{9,8},{10,9},{11,10},{13,12},{... | collective-permute-start | bytes 3145736 | tf_op jit(solution)/shard_map/ppermute | solution.py:289
  426.7 124.6 %reduce-scatter.15.cloned.1.call-start = ((), (), s32[]{:S(2)}) async-start(), calls=%async_computation.12 | async-start | bytes 1310720 | tf_op jit(solution)/shard_map/reduce_scatter | solution.py:165
  430.0 149.4 %reduce-scatter.17.cloned.1.call-start = ((), (), s32[]{:S(2)}) async-start(), calls=%async_computation.13 | async-start | bytes 1310720 | tf_op jit(solution)/shard_map/reduce_scatter | solution.py:165
  448.0 176.3 %reduce-scatter.11.cloned.1.call-start = ((), (), s32[]{:S(2)}) async-start(), calls=%async_computation.10 | async-start | bytes 2621440 | tf_op jit(solution)/shard_map/reduce_scatter | solution.py:329
  (34 other events, 503.8 us)
Sparse Core Ops, SparseCore 0:
  11.8 32.8 all-gather.17
  46.3 26.2 all-gather.19
  74.7 27.4 all-gather.21
  104.5 55.5 all-gather.11
  161.8 55.9 all-gather.13
  219.6 55.9 all-gather.15
  299.2 71.2 reduce-scatter.12
  374.4 71.2 reduce-scatter.18
  449.3 72.6 reduce-scatter.8
  524.2 27.1 reduce-scatter.14
  553.6 25.7 reduce-scatter.16
  581.7 42.5 reduce-scatter.10

commit v2 on v1

--- a/solution.py
+++ b/solution.py
@@ -147,14 +147,41 @@
     )(query, keys, values, far, grad, lse)
 
 
-def gather_plane(parts):
-    count = len(parts)
-    rows, width = parts[0].shape
-    packed = jnp.concatenate(parts, axis=1)
-    lines = lax.all_gather(packed, "tensor", axis=0, tiled=False)
-    tensor = lines.shape[0]
-    lines = lines.reshape(tensor, rows, count, width).transpose(1, 2, 0, 3)
-    lines = lines.reshape(rows, count * tensor * width)
+def shift_by(value, step):
+    size = lax.axis_size("tensor")
+    return lax.ppermute(value, "tensor", [(i, (i + step) % size) for i in range(size)])
+
+
+def gather_line(value):
+    size = lax.axis_size("tensor")
+    place = lax.axis_index("tensor")
+    arrived = [value] + [shift_by(value, step) for step in range(1, size)]
+    ordered = jnp.stack(arrived[::-1] * 2)
+    return lax.dynamic_slice_in_dim(ordered, (2 * size - 1 - place) % size, size)
+
+
+def sum_line(split):
+    size = lax.axis_size("tensor")
+    place = lax.axis_index("tensor")
+    total = lax.dynamic_index_in_dim(split, place, keepdims=False).astype(F32)
+    for step in range(1, size):
+        sent = lax.dynamic_index_in_dim(split, (place + step) % size, keepdims=False)
+        total = total + shift_by(sent, step).astype(F32)
+    return total
+
+
+def merge_line(lines, count):
+    tensor, rows, columns = lines.shape
+    lines = lines.reshape(tensor, rows, count, columns // count).transpose(1, 2, 0, 3)
+    return lines.reshape(rows, tensor * columns)
+
+
+def after(arrived, value):
+    token = arrived[(0,) * arrived.ndim]
+    return jnp.where(jnp.isnan(token), jnp.zeros_like(value), value)
+
+
+def gather_rows(lines):
     return lax.all_gather(lines, "dp", axis=0, tiled=True)
 
 
@@ -162,8 +189,8 @@
     rows = summed.shape[0]
     tensor = lax.axis_size("tensor")
     split = summed.reshape(rows, count, tensor, -1).transpose(2, 0, 1, 3)
-    own = lax.psum_scatter(split, "tensor", scatter_dimension=0, tiled=False)
-    return [own[:, i, :].astype(F32) for i in range(count)]
+    own = sum_line(split)
+    return [own[:, i, :] for i in range(count)]
 
 
 def scatter_plane(grads):
@@ -197,8 +224,6 @@
     onward = [(i, i + 1) for i in range(tensor - 1)]
     backward = [(i + 1, i) for i in range(tensor - 1)]
 
-    halo = lax.ppermute(block_input, "tensor", onward)
-
     small = jnp.concatenate(
         [
             ln1_gain,
@@ -216,8 +241,30 @@
     piece = ln1_gain.shape[0]
     hidden_piece = fc1_bias.shape[0]
     padded = -(-small_width // 128) * 128
-    small = jnp.pad(small, (0, padded - small_width))[None]
-    vectors = lax.all_gather(small, ("dp", "tensor"), axis=0, tiled=True).astype(F32)
+
+    attn_local = jnp.concatenate([w_query, w_key, w_value, w_dense.T], axis=1)
+    block_width, attn_width = attn_local.shape
+    lanes = 128 * -(-(tensor * padded) // (128 * block_width))
+    small = jnp.pad(small, (0, 16 * attn_width - small_width)).reshape(16, attn_width)
+    first_lines = lax.all_gather(
+        jnp.concatenate([attn_local, small], axis=0), "tensor", axis=0, tiled=False
+    )
+    small_lines = first_lines[:, block_width:].reshape(tensor, -1)[:, :padded].reshape(-1)
+    small_lines = jnp.pad(small_lines, (0, block_width * lanes - tensor * padded))
+    attn_lines = jnp.concatenate(
+        [merge_line(first_lines[:, :block_width], 4), small_lines.reshape(block_width, lanes)],
+        axis=1,
+    )
+    attn_weights = gather_rows(attn_lines)
+
+    halo = lax.ppermute(after(first_lines, block_input), "tensor", onward)
+    fc1_lines = merge_line(gather_line(after(first_lines, w_fc1)), 1)
+    fc2_lines = merge_line(gather_line(after(first_lines, w_fc2.T)), 1)
+    ffn_first = gather_rows(after(attn_weights, fc1_lines))
+    ffn_second = gather_rows(after(ffn_first, fc2_lines))
+
+    vectors = attn_weights[:, 4 * width :].reshape(dp, block_width * lanes)[:, : tensor * padded]
+    vectors = vectors.reshape(dp * tensor, padded).astype(F32)
     pieces = [piece] * 7 + [hidden_piece, piece]
     starts = [sum(pieces[:i]) for i in range(len(pieces))]
     (
@@ -232,11 +279,8 @@
         output_shift,
     ) = [vectors[:, s : s + n].reshape(-1) for s, n in zip(starts, pieces)]
 
-    attn_weights = gather_plane([w_query, w_key, w_value, w_dense.T])
-    ffn_first = gather_plane([w_fc1])
-    ffn_second = gather_plane([w_fc2.T])
     qkv_weights = attn_weights[:, : 3 * width]
-    dense_t = attn_weights[:, 3 * width :]
+    dense_t = attn_weights[:, 3 * width : 4 * width]
 
     extended = jnp.concatenate([halo, block_input], axis=0).astype(F32)
     unit_first, inverse_first = norm_parts(extended)
@@ -304,8 +348,6 @@
     shares = [g.reshape(dp, tensor, -1) for g in small_grads]
     shares = jnp.concatenate(shares, axis=2)
     shares = jnp.pad(shares, ((0, 0), (0, 0), (0, padded - small_width)))
-    block_width = width // dp
-    lanes = 128 * -(-(tensor * padded) // (128 * block_width))
     shares = shares.reshape(dp, tensor * padded)
     shares = jnp.pad(shares, ((0, 0), (0, block_width * lanes - tensor * padded)))
     shares = shares.reshape(width, lanes).astype(BF)
@@ -323,7 +365,7 @@
     split = split.reshape(tensor, block_width, -1)
     small_sum = last_sum[:, 4 * width :].reshape(-1)[: tensor * padded].reshape(tensor, padded)
     extra = split.shape[2]
-    small_rows = -(-padded // extra)
+    small_rows = 16 * -(-padded // (16 * extra))
     small_sum = jnp.pad(small_sum, ((0, 0), (0, small_rows * extra - padded)))
     split = jnp.concatenate([split, small_sum.reshape(tensor, small_rows, extra)], axis=1)
     own = lax.psum_scatter(split, "tensor", scatter_dimension=0, tiled=False)

time: 646 us -> 690 us (1.068)
  waiting for transfers between devices: 279 us -> 364 us
  blocking collectives: 83.8 us -> 0 us
  starting transfers between devices: 7.03 us -> 25.8 us
  local copies, waits for them, and re-layouts: 53.7 us -> 65.6 us
  matrix products: 110 us -> 118 us
    ppermute x1 -> x13, waiting for transfers between devices: 0.01 us -> 113 us  [the longest x12 92.4 us: shift_by(): lax.ppermute(value, 'tensor', [(i, (i + step) % size) for i in range(size)])]
    all_gather x1 -> x0, blocking collectives: 83.8 us -> none  [per_device(): lax.all_gather(small, ('dp', 'tensor'), axis=0, tiled=True).astype(F32)]
    reduce_scatter x1, waiting for transfers between devices: 43 us -> 0.01 us  [per_device(): own = lax.psum_scatter(split, 'tensor', scatter_dimension=0, tiled=False)]
    unnamed x13 -> x9, waiting for transfers between devices: 16.5 us -> 52.1 us
    reduce_scatter x2 -> x0, waiting for transfers between devices: 30.8 us -> none  [scatter_line(): own = lax.psum_scatter(split, 'tensor', scatter_dimension=0, tiled=False)]
    reduce_scatter x2, waiting for transfers between devices: 73.5 us -> 104 us  [scatter_plane(): return lax.psum_scatter(grads, 'dp', scatter_dimension=0, tiled=True)]
    all_gather x6 -> x4, waiting for transfers between devices: 107 us -> 86 us  [the longest x3 52.7 us: gather_rows(): return lax.all_gather(lines, 'dp', axis=0, tiled=True)]
    ppermute x1 -> x13, starting transfers between devices: 4.36 us -> 23.8 us  [the longest x12 19.4 us: shift_by(): lax.ppermute(value, 'tensor', [(i, (i + step) % size) for i in range(size)])]
  transfers between devices with their start and end apart: 14 -> 22, of which waited for: 10 -> 13; matrix products, arithmetic and copies ran while one was open for 25% -> 19% of each run, Pallas kernels for 9% -> 3%
where the time goes in v2:
time: 690 us; the launch traced here: 683 us
  waiting for transfers between devices  364 us (53%)
  matrix products  118 us (17%)
  local copies, waits for them, and re-layouts  65.6 us (10%)
  Pallas kernels  55 us (8%)
  other arithmetic  35.6 us (5%)
  starting transfers between devices  25.8 us (4%)
  between operations  19.1 us (3%)
    dot_general x15, matrix products, dot(): lax.dot_general(left, right, (((left_dim,), (right_dim,)), ((), ())), pre...  118 us
    reduce_scatter x2, waiting for transfers between devices, scatter_plane(): return lax.psum_scatter(grads, 'dp', scatter_dimension=0, tiled=True)  104 us
    ppermute x12, waiting for transfers between devices, shift_by(): lax.ppermute(value, 'tensor', [(i, (i + step) % size) for i in range(size)])  92.4 us
    all_gather x3, waiting for transfers between devices, gather_rows(): return lax.all_gather(lines, 'dp', axis=0, tiled=True)  52.7 us
    unnamed x9, waiting for transfers between devices  52.1 us
    pallas_call x1, Pallas kernels, attend_back(): pl.pallas_call(attend_back_kernel, grid=(pairs,), in_specs=[column, tall,...  34.2 us
    all_gather x1, waiting for transfers between devices, per_device(): lax.all_gather(jnp.concatenate([attn_local, small], axis=0), 'tensor', ax...  33.2 us
    unnamed x99, local copies, waits for them, and re-layouts  28.6 us
  transfers between devices with their start and end apart: 22, of which 13 were waited for; matrix products, arithmetic and copies ran while one was open for 19% of the time, Pallas kernels for 3%

profile of v2, /device:TPU:0, one launch (start us, length us, event | category | flops | bytes accessed | tf_op | source)
XLA Modules:
  0.0 683.1 jit_solution(13495807391544077866)
XLA Ops:
  16.0 33.2 %all-gather.12.cloned.1.call-done = bf16[576,1024]{1,0:T(8,128)(2,1)} async-done(((bf16[144,1024]{1,0:T(8,128)(2,1)}), bf16[576,1024]{1,0:T(8,128)(2,1)}) %all-gather.12.cloned.1.call-update) | async-done | bytes 1179664 | tf_op jit(solution)/shard_map/all_gather | solution.py:249
  65.6 16.7 %collective-permute-done.2 = bf16[128,1024]{0,1:T(8,128)(2,1)S(1)} collective-permute-done((bf16[128,1024]{0,1:T(8,128)(2,1)S(1)}, bf16[128,1024]{0,1:T(8,128)(2,1)S(1)}, u32[]{:S(2)}, u32[]{:S(2)}) %collective-permute-start.2) | collective-permute-done | bytes 262176 | tf_op jit(solution)/shard_map/ppermute | solution.py:152
  82.8 28.1 %all-gather.6.cloned.1.call-done = bf16[1024,4224]{0,1:T(8,128)(2,1)} async-done(((bf16[128,4224]{0,1:T(8,128)(2,1)}), bf16[1024,4224]{0,1:T(8,128)(2,1)}) %all-gather.6.cloned.1.call-update) | async-done | bytes 8650768 | tf_op jit(solution)/shard_map/all_gather | solution.py:185
  125.4 15.5 %collective-permute-done.5 = bf16[128,1024]{0,1:T(8,128)(2,1)S(1)} collective-permute-done((bf16[128,1024]{0,1:T(8,128)(2,1)S(1)}, bf16[128,1024]{0,1:T(8,128)(2,1)S(1)}, u32[]{:S(2)}, u32[]{:S(2)}) %collective-permute-start.5) | collective-permute-done | bytes 262176 | tf_op jit(solution)/shard_map/ppermute | solution.py:152
  145.9 24.6 %all-gather.8.cloned.1.call-done = bf16[1024,4096]{0,1:T(8,128)(2,1)} async-done(((bf16[128,4096]{0,1:T(8,128)(2,1)}), bf16[1024,4096]{0,1:T(8,128)(2,1)}) %all-gather.8.cloned.1.call-update) | async-done | bytes 8388624 | tf_op jit(solution)/shard_map/all_gather | solution.py:185
  182.5 20.4 %collective-permute-done = bf16[512,1024]{1,0:T(8,128)(2,1)} collective-permute-done((bf16[512,1024]{1,0:T(8,128)(2,1)}, bf16[512,1024]{1,0:T(8,128)(2,1)}, u32[]{:S(2)}, u32[]{:S(2)}) %collective-permute-start) | collective-permute-done | bytes 1048608 | tf_op jit(solution)/shard_map/ppermute | solution.py:260
  216.4 7.9 %add_convert_fusion = bf16[1024,2048]{1,0:T(8,128)(2,1)S(1)} fusion(f32[2048]{0:T(1024)S(1)} %concatenate.36, bf16[1024,1024]{1,0:T(8,128)(2,1)S(1)} %get-tuple-element.46, bf16[1024,4224]{0,1:T(8,128)(2,1)} %all-gather.6.cloned.1.call-done), kind=kOutput, calls=%fused_computation.17 | convolution fusion | flops 4299161600 | bytes 10493952 | tf_op jit(solution)/shard_map/dot_general | solution.py:41
  229.4 20.8 %shard_map.305 = (bf16[512,1024]{1,0:T(8,128)(2,1)S(1)}, f32[16,512,1]{2,1,0:T(8,128)S(1)}) custom-call(bf16[512,1024]{1,0:T(8,128)(2,1)S(1)} %fusion.36.q_ref, bf16[1024,1024]{1,0:T(8,128)(2,1)S(1)} %get-tuple-element.44.k_ref, bf16[1024,1024]{1,0:T(8,128)(2,1)S(1)} %get-tuple-element.43.v_ref, f32[512,1024]{1,0:T(8,128)S(1)} %fusion.16.far_ref), custom_call_target="tpu_custom_call" | custom-call | flops 40000000000 | bytes 20000000 | tf_op jit(solution)/shard_map/pallas_call | solution.py:108
  256.5 7.4 %fusion.61 = f32[4096,512]{0,1:T(8,128)S(1)} fusion(bf16[1024,4096]{0,1:T(8,128)(2,1)} %all-gather.10.cloned.1.call-done, bf16[512,1024]{1,0:T(8,128)(2,1)} %param.34), kind=kOutput, calls=%fused_computation.148 | convolution fusion | flops 4294967296 | bytes 17825792 | tf_op jit(solution)/shard_map/dot_general | solution.py:41
  263.9 15.3 %fusion.52 = (bf16[4096]{0:T(1024)(128)(2,1)S(1)}, bf16[512,4096]{1,0:T(8,128)(2,1)}, f32[512,4096]{1,0:T(8,128)}) fusion(f32[4096]{0:T(1024)S(1)} %slice_bitcast_fusion.1, f32[4096,512]{0,1:T(8,128)S(1)} %fusion.61, bf16[1024,4096]{0,1:T(8,128)(2,1)} %all-gather.8.cloned.1.call-done, f32[512,1024]{1,0:T(8,128)S(1)} %copy-done.12, f32[1024]{0:T(1024)S(1)} %add.256, ...), kind=kOutput, calls=%fused_computation.140 | convolution fusion | flops 4343721984 | bytes 31494144 | tf_op jit(solution)/shard_map/dot_general | solution.py:41
  279.2 8.8 %multiply_reduce_fusion = (bf16[1024]{0:T(1024)(128)(2,1)S(1)}, f32[512]{0:T(512)S(1)}, f32[512]{0:T(512)S(1)}, bf16[1024]{0:T(1024)(128)(2,1)S(1)}, f32[512,1024]{1,0:T(8,128)S(1)}) fusion(f32[512,1024]{1,0:T(8,128)S(1)} %copy-done.12, f32[512]{0:T(512)S(1)} %add_rsqrt_fusion.1, f32[512]{0:T(512)S(1)} %broadcast_multiply_fusion.5, f32[1024]{0:T(1024)S(1)} %mul.166, ...), kind=kOutput, calls=%fused_computation.36 | convolution fusion | flops 4299682816 | bytes 16793600 | tf_op jit(solution)/shard_map/dot_general | solution.py:41
  294.6 34.2 %shard_map.306 = (bf16[512,1024]{1,0:T(8,128)(2,1)S(1)}, bf16[1024,1024]{1,0:T(8,128)(2,1)S(1)}, bf16[1024,1024]{1,0:T(8,128)(2,1)S(1)}) custom-call(bf16[512,1024]{1,0:T(8,128)(2,1)S(1)} %copy-done.5, bf16[1024,1024]{1,0:T(8,128)(2,1)S(1)} %copy-done.3, bf16[1024,1024]{1,0:T(8,128)(2,1)S(1)} %copy-done.1, f32[512,1024]{1,0:T(8,128)S(1)} %fusion.16.far_ref, ...), custom_call_target="tpu_custom_call" | custom-call | flops 80000000000 | bytes 30000000 | tf_op jit(solution)/shard_map/pallas_call | solution.py:132
  329.7 7.8 %fusion.13 = f32[1024,1024]{1,0:T(8,128)S(1)} fusion(bf16[1024,2048]{1,0:T(8,128)(2,1)S(1)} %get-tuple-element.48, bf16[1024,4224]{0,1:T(8,128)(2,1)} %all-gather.6.cloned.1.call-done), kind=kOutput, calls=%fused_computation.26 | convolution fusion | flops 4294967296 | bytes 12582912 | tf_op jit(solution)/shard_map/dot_general | solution.py:41
  348.0 9.6 %convolution_convert_fusion.1 = bf16[1024,2048]{1,0:T(8,128)(2,1)} fusion(bf16[1024,1024]{1,0:T(8,128)(2,1)} %copy-done.20, bf16[1024,2048]{1,0:T(8,128)(2,1)} %copy-done.22), kind=kOutput, calls=%fused_computation.25 | convolution fusion | flops 4297064448 | bytes 10485760 | tf_op jit(solution)/shard_map/dot_general | solution.py:41
  357.5 9.9 %collective-permute-done.7 = bf16[512,1024]{1,0:T(8,128)(2,1)} collective-permute-done((bf16[512,1024]{1,0:T(8,128)(2,1)}, bf16[512,1024]{1,0:T(8,128)(2,1)}, u32[]{:S(2)}, u32[]{:S(2)}) %collective-permute-start.7) | collective-permute-done | bytes 1048608 | tf_op jit(solution)/shard_map/ppermute | solution.py:333
  373.4 6.6 pad_maximum_fusion
  381.2 14.1 %convert_bitcast_fusion = bf16[1024,4096]{0,1:T(8,128)(2,1)} fusion(bf16[512,1024]{1,0:T(8,128)(2,1)S(1)} %copy-done.18, f32[512,4096]{1,0:T(8,128)} %get-tuple-element.78, f32[4096]{0:T(1024)S(1)} %slice_bitcast_fusion.1), kind=kOutput, calls=%fused_computation.15 | convolution fusion | flops 4320133120 | bytes 17842176 | tf_op jit(solution)/shard_map/dot_general | solution.py:41
  395.3 11.3 %copy.126 = bf16[1024,4096]{1,0:T(8,128)(2,1)} copy(bf16[1024,4096]{0,1:T(8,128)(2,1)} %convert_bitcast_fusion) | data formatting | bytes 16777216
  408.2 9.2 %convolution_convert_fusion = bf16[1024,4096]{1,0:T(8,128)(2,1)} fusion(bf16[512,4096]{1,0:T(8,128)(2,1)} %get-tuple-element.40, f32[512,1024]{1,0:T(8,128)S(1)} %copy-done.13, f32[1024]{0:T(1024)S(1)} %copy-done.33, f32[1024]{0:T(1024)S(1)} %mul.166, f32[512]{0:T(512)S(1)} %add_rsqrt_fusion.1, f32[512]{0:T(512)S(1)} %broadcast_multiply_fusion.5), kind=kOutput, calls=%fused_computation.18 | convolution fusion | flops 4301783040 | bytes 14692352 | tf_op jit(solution)/shard_map/dot_general | solution.py:41
  418.2 33.9 %reduce-scatter.7.cloned.1.call-done = bf16[128,4224]{1,0:T(8,128)(2,1)} async-done(((bf16[1024,4224]{1,0:T(8,128)(2,1)}), bf16[128,4224]{1,0:T(8,128)(2,1)}) %reduce-scatter.7.cloned.1.call-update) | async-done | bytes 1081360 | tf_op jit(solution)/shard_map/reduce_scatter | solution.py:197
  460.2 14.9 %add_convert_fusion.2 = bf16[512,1024]{1,0:T(8,128)(2,1)} fusion(f32[512,1024]{1,0:T(8,128)S(1)} %copy-done.13, bf16[1024,4096]{0,1:T(8,128)(2,1)} %all-gather.10.cloned.1.call-done, f32[1024]{0:T(1024)S(1)} %add.267, f32[512,4096]{1,0:T(8,128)} %get-tuple-element.78, f32[4096]{0:T(1024)S(1)} %slice_bitcast_fusion.1), kind=kOutput, calls=%fused_computation.43 | convolution fusion | flops 4317511680 | bytes 19943424 | tf_op jit(solution)/shard_map/dot_general | solution.py:41
  475.1 52.0 %reduce-scatter.13.cloned.1.call-done = bf16[128,4096]{1,0:T(8,128)(2,1)} async-done(((bf16[1024,4096]{1,0:T(8,128)(2,1)}), bf16[128,4096]{1,0:T(8,128)(2,1)}) %reduce-scatter.13.cloned.1.call-update) | async-done | bytes 1048592
  532.2 69.7 %reduce-scatter.11.cloned.1.call-done = bf16[128,4096]{1,0:T(8,128)(2,1)} async-done(((bf16[1024,4096]{1,0:T(8,128)(2,1)}), bf16[128,4096]{1,0:T(8,128)(2,1)}) %reduce-scatter.11.cloned.1.call-update) | async-done | bytes 1048592 | tf_op jit(solution)/shard_map/reduce_scatter | solution.py:197
  617.9 49.8 %collective-permute-done.12 = bf16[128,1,1024]{0,2,1:T(8,128)(2,1)S(1)} collective-permute-done((bf16[128,1,1024]{0,2,1:T(8,128)(2,1)S(1)}, bf16[128,1,1024]{0,2,1:T(8,128)(2,1)S(1)}, u32[]{:S(2)}, u32[]{:S(2)}) %collective-permute-start.12) | collective-permute-done | bytes 262176 | tf_op jit(solution)/shard_map/ppermute | solution.py:152
  (245 shorter events, 142.3 us)
Async XLA Ops:
  7.2 42.1 %all-gather.12.cloned.1.call-start = ((), (), s32[]{:S(2)}) async-start(), calls=%async_computation.10 | async-start | bytes 1474560 | tf_op jit(solution)/shard_map/all_gather | solution.py:249
  16.0 94.9 %all-gather.6.cloned.1.call-start = ((), (), s32[]{:S(2)}) async-start(), calls=%async_computation.4 | async-start | bytes 9732096 | tf_op jit(solution)/shard_map/all_gather | solution.py:185
  54.5 116.1 %all-gather.8.cloned.1.call-start = ((), (), s32[]{:S(2)}) async-start(), calls=%async_computation.5 | async-start | bytes 9437184 | tf_op jit(solution)/shard_map/all_gather | solution.py:185
  57.2 8.4 %collective-permute-start.1 = (bf16[128,1024]{0,1:T(8,128)(2,1)S(1)}, bf16[128,1024]{0,1:T(8,128)(2,1)S(1)}, u32[]{:S(2)}, u32[]{:S(2)}) collective-permute-start(bf16[128,1024]{0,1:T(8,128)(2,1)S(1)} %broadcast_select_fusion.2), channel_id=1, source_target_pairs={{0,3},{1,0},{2,1},{3,2},{4,7},{5,4},{6,5},{7,6},{8,11},{9,8},{10,9... | collective-permute-start | bytes 786440 | tf_op jit(solution)/shard_map/ppermute | solution.py:152
  58.8 23.6 %collective-permute-start.2 = (bf16[128,1024]{0,1:T(8,128)(2,1)S(1)}, bf16[128,1024]{0,1:T(8,128)(2,1)S(1)}, u32[]{:S(2)}, u32[]{:S(2)}) collective-permute-start(bf16[128,1024]{0,1:T(8,128)(2,1)S(1)} %broadcast_select_fusion.2), channel_id=1, source_target_pairs={{0,2},{1,3},{2,0},{3,1},{4,6},{5,7},{6,4},{7,5},{8,10},{9,11},{10,... | collective-permute-start | bytes 786440 | tf_op jit(solution)/shard_map/ppermute | solution.py:152
  59.7 22.7 %collective-permute-start.3 = (bf16[128,1024]{0,1:T(8,128)(2,1)S(1)}, bf16[128,1024]{0,1:T(8,128)(2,1)S(1)}, u32[]{:S(2)}, u32[]{:S(2)}) collective-permute-start(bf16[128,1024]{0,1:T(8,128)(2,1)S(1)} %broadcast_select_fusion.2), channel_id=1, source_target_pairs={{0,1},{1,2},{2,3},{3,0},{4,5},{5,6},{6,7},{7,4},{8,9},{9,10},{10,1... | collective-permute-start | bytes 786440 | tf_op jit(solution)/shard_map/ppermute | solution.py:152
  82.6 31.8 %copy-start.19 = (bf16[1024,128]{1,0:T(8,128)(2,1)S(1)}, bf16[1024,128]{1,0:T(8,128)(2,1)}, u32[]{:S(2)}) copy-start(bf16[1024,128]{1,0:T(8,128)(2,1)} %param.32) | copy-start | bytes 786436
  114.4 142.1 %all-gather.10.cloned.1.call-start = ((), (), s32[]{:S(2)}) async-start(), calls=%async_computation.6 | async-start | bytes 9437184 | tf_op jit(solution)/shard_map/all_gather | solution.py:185
  114.5 10.1 %collective-permute-start.4 = (bf16[128,1024]{0,1:T(8,128)(2,1)S(1)}, bf16[128,1024]{0,1:T(8,128)(2,1)S(1)}, u32[]{:S(2)}, u32[]{:S(2)}) collective-permute-start(bf16[128,1024]{0,1:T(8,128)(2,1)S(1)} %fusion.50), channel_id=1, source_target_pairs={{0,3},{1,0},{2,1},{3,2},{4,7},{5,4},{6,5},{7,6},{8,11},{9,8},{10,9... | collective-permute-start | bytes 786440 | tf_op jit(solution)/shard_map/ppermute | solution.py:152
  117.9 22.9 %collective-permute-start.5 = (bf16[128,1024]{0,1:T(8,128)(2,1)S(1)}, bf16[128,1024]{0,1:T(8,128)(2,1)S(1)}, u32[]{:S(2)}, u32[]{:S(2)}) collective-permute-start(bf16[128,1024]{0,1:T(8,128)(2,1)S(1)} %fusion.50), channel_id=1, source_target_pairs={{0,2},{1,3},{2,0},{3,1},{4,6},{5,7},{6,4},{7,5},{8,10},{9,11},{10,... | collective-permute-start | bytes 786440 | tf_op jit(solution)/shard_map/ppermute | solution.py:152
  117.9 23.6 %collective-permute-start.6 = (bf16[128,1024]{0,1:T(8,128)(2,1)S(1)}, bf16[128,1024]{0,1:T(8,128)(2,1)S(1)}, u32[]{:S(2)}, u32[]{:S(2)}) collective-permute-start(bf16[128,1024]{0,1:T(8,128)(2,1)S(1)} %fusion.50), channel_id=1, source_target_pairs={{0,1},{1,2},{2,3},{3,0},{4,5},{5,6},{6,7},{7,4},{8,9},{9,10},{10,1... | collective-permute-start | bytes 786440 | tf_op jit(solution)/shard_map/ppermute | solution.py:152
  175.3 276.8 %reduce-scatter.7.cloned.1.call-start = ((), (), s32[]{:S(2)}) async-start(), calls=%async_computation.7 | async-start | bytes 9732096 | tf_op jit(solution)/shard_map/reduce_scatter | solution.py:197
  176.4 26.5 %collective-permute-start = (bf16[512,1024]{1,0:T(8,128)(2,1)}, bf16[512,1024]{1,0:T(8,128)(2,1)}, u32[]{:S(2)}, u32[]{:S(2)}) collective-permute-start(bf16[512,1024]{1,0:T(8,128)(2,1)} %broadcast_select_fusion), channel_id=1, source_target_pairs={{0,1},{1,2},{2,3},{4,5},{5,6},{6,7},{8,9},{9,10},{10,11},{12,13},{... | collective-permute-start | bytes 3145736 | tf_op jit(solution)/shard_map/ppermute | solution.py:260
  212.3 51.6 %copy-start.32 = (f32[1024]{0:T(1024)}, f32[1024]{0:T(1024)S(1)}, u32[]{:S(2)}) copy-start(f32[1024]{0:T(1024)S(1)} %add.256) | copy-start | bytes 12292
  340.0 27.4 %collective-permute-start.7 = (bf16[512,1024]{1,0:T(8,128)(2,1)}, bf16[512,1024]{1,0:T(8,128)(2,1)}, u32[]{:S(2)}, u32[]{:S(2)}) collective-permute-start(bf16[512,1024]{1,0:T(8,128)(2,1)} %slice.287), channel_id=1, source_target_pairs={{1,0},{2,1},{3,2},{5,4},{6,5},{7,6},{9,8},{10,9},{11,10},{13,12},{... | collective-permute-start | bytes 3145736 | tf_op jit(solution)/shard_map/ppermute | solution.py:333
  380.0 147.1 %reduce-scatter.13.cloned.1.call-start = ((), (), s32[]{:S(2)}) async-start(), calls=%async_computation.11 | async-start | bytes 9437184
  406.6 195.3 %reduce-scatter.11.cloned.1.call-start = ((), (), s32[]{:S(2)}) async-start(), calls=%async_computation.9 | async-start | bytes 9437184 | tf_op jit(solution)/shard_map/reduce_scatter | solution.py:197
  417.4 252.2 %reduce-scatter.9.cloned.1.call-start = ((), (), s32[]{:S(2)}) async-start(), calls=%async_computation.8 | async-start | bytes 1474560 | tf_op jit(solution)/shard_map/reduce_scatter | solution.py:371
  528.8 83.9 %collective-permute-start.13 = (bf16[128,1,1024]{0,2,1:T(8,128)(2,1)S(1)}, bf16[128,1,1024]{0,2,1:T(8,128)(2,1)S(1)}, u32[]{:S(2)}, u32[]{:S(2)}) collective-permute-start(bf16[128,1,1024]{0,2,1:T(8,128)(2,1)S(1)} %get-tuple-element.50), channel_id=1, source_target_pairs={{0,3},{1,0},{2,1},{3,2},{4,7},{5,4},{6,5},{7,6},{8,11},{9,8},{10,9... | collective-permute-start | bytes 786440 | tf_op jit(solution)/shard_map/ppermute | solution.py:152
  606.0 62.6 %collective-permute-start.10 = (bf16[128,1,1024]{2,0,1:T(8,128)(2,1)S(1)}, bf16[128,1,1024]{2,0,1:T(8,128)(2,1)S(1)}, u32[]{:S(2)}, u32[]{:S(2)}) collective-permute-start(bf16[128,1,1024]{2,0,1:T(8,128)(2,1)S(1)} %bitcast.153), channel_id=1, source_target_pairs={{0,3},{1,0},{2,1},{3,2},{4,7},{5,4},{6,5},{7,6},{8,11},{9,8},{10,9... | collective-permute-start | bytes 786440 | tf_op jit(solution)/shard_map/ppermute | solution.py:152
  609.5 59.1 %collective-permute-start.9 = (bf16[128,1,1024]{2,0,1:T(8,128)(2,1)S(1)}, bf16[128,1,1024]{2,0,1:T(8,128)(2,1)S(1)}, u32[]{:S(2)}, u32[]{:S(2)}) collective-permute-start(bf16[128,1,1024]{2,0,1:T(8,128)(2,1)S(1)} %bitcast.154), channel_id=1, source_target_pairs={{0,2},{1,3},{2,0},{3,1},{4,6},{5,7},{6,4},{7,5},{8,10},{9,11},{10,... | collective-permute-start | bytes 786440 | tf_op jit(solution)/shard_map/ppermute | solution.py:152
  609.7 59.0 %collective-permute-start.8 = (bf16[128,1,1024]{2,0,1:T(8,128)(2,1)S(1)}, bf16[128,1,1024]{2,0,1:T(8,128)(2,1)S(1)}, u32[]{:S(2)}, u32[]{:S(2)}) collective-permute-start(bf16[128,1,1024]{2,0,1:T(8,128)(2,1)S(1)} %bitcast.155), channel_id=1, source_target_pairs={{0,1},{1,2},{2,3},{3,0},{4,5},{5,6},{6,7},{7,4},{8,9},{9,10},{10,1... | collective-permute-start | bytes 786440 | tf_op jit(solution)/shard_map/ppermute | solution.py:152
  610.8 56.9 %collective-permute-start.12 = (bf16[128,1,1024]{0,2,1:T(8,128)(2,1)S(1)}, bf16[128,1,1024]{0,2,1:T(8,128)(2,1)S(1)}, u32[]{:S(2)}, u32[]{:S(2)}) collective-permute-start(bf16[128,1,1024]{0,2,1:T(8,128)(2,1)S(1)} %get-tuple-element.51), channel_id=1, source_target_pairs={{0,2},{1,3},{2,0},{3,1},{4,6},{5,7},{6,4},{7,5},{8,10},{9,11},{10,... | collective-permute-start | bytes 786440 | tf_op jit(solution)/shard_map/ppermute | solution.py:152
  612.7 55.0 %collective-permute-start.11 = (bf16[128,1,1024]{0,2,1:T(8,128)(2,1)S(1)}, bf16[128,1,1024]{0,2,1:T(8,128)(2,1)S(1)}, u32[]{:S(2)}, u32[]{:S(2)}) collective-permute-start(bf16[128,1,1024]{0,2,1:T(8,128)(2,1)S(1)} %get-tuple-element.49), channel_id=1, source_target_pairs={{0,1},{1,2},{2,3},{3,0},{4,5},{5,6},{6,7},{7,4},{8,9},{9,10},{10,1... | collective-permute-start | bytes 786440 | tf_op jit(solution)/shard_map/ppermute | solution.py:152
  (34 other events, 254.2 us)
Sparse Core Ops, SparseCore 0:
  16.1 33.1 all-gather.11
  54.6 56.2 all-gather.5
  114.5 55.9 all-gather.7
  175.4 55.9 all-gather.9
  380.1 71.9 reduce-scatter.6
  455.8 71.2 reduce-scatter.12
  530.6 71.2 reduce-scatter.10
  604.3 57.7 reduce-scatter.8
